TPU v7x, 32 devices: a whole 2x2x4 slice. The times are simulated.
32 devices in a mesh: dp: 8 (over z, x), tensor: 4 (over y, core).
Axes of the slice: x: 2, y: 2, z: 4, core: 2. Of those that a mesh axis runs over, the one named last changes fastest.
Arguments:
- media: bfloat16 [24, 2048, 1024], P('dp'), may hold values from -6 to 6
- frame_counts: int32 [24], P('dp'), may hold values from 1 to 8, as said below
- time_embed: bfloat16 [8, 1024], replicated, may hold values from -3 to 3
- latents: bfloat16 [64, 1024], replicated, may hold values from -6 to 6
- media_gain: float32 [2, 1024], replicated, may hold values from 0.5 to 1.5
- media_bias: float32 [2, 1024], replicated, may hold values from -1.75 to 1.75
- latent_gain: float32 [2, 1024], replicated, may hold values from 0.5 to 1.5
- latent_bias: float32 [2, 1024], replicated, may hold values from -1.75 to 1.75
- ff_gain: float32 [2, 1024], replicated, may hold values from 0.5 to 1.5
- ff_bias: float32 [2, 1024], replicated, may hold values from -1.75 to 1.75
- w_query: bfloat16 [2, 1024, 512], P(None, None, 'tensor'), may hold values from -0.375 to 0.375
- w_key: bfloat16 [2, 1024, 512], P(None, None, 'tensor'), may hold values from -0.1875 to 0.1875
- w_value: bfloat16 [2, 1024, 512], P(None, None, 'tensor'), may hold values from -0.1875 to 0.1875
- w_out: bfloat16 [2, 512, 1024], P(None, 'tensor'), may hold values from -3 to 3
- w_up: bfloat16 [2, 1024, 4096], P(None, None, 'tensor'), may hold values from -0.1875 to 0.1875
- w_down: bfloat16 [2, 4096, 1024], P(None, 'tensor'), may hold values from -0.09375 to 0.09375
- cotangent: float32 [24, 64, 1024], P('dp'), may hold values from -6 to 6
Outputs:
- resampled: float32 [24, 64, 1024], P('dp')
- media_grad: bfloat16 [24, 2048, 1024], P('dp', None, 'tensor')
- time_grad: float32 [8, 1024], replicated
- latents_grad: float32 [64, 1024], replicated
- media_gain_grad: float32 [2, 1024], replicated
- media_bias_grad: float32 [2, 1024], replicated
- latent_gain_grad: float32 [2, 1024], replicated
- latent_bias_grad: float32 [2, 1024], replicated
- ff_gain_grad: float32 [2, 1024], replicated
- ff_bias_grad: float32 [2, 1024], replicated
- w_query_grad: float32 [2, 1024, 512], P(None, 'dp', 'tensor')
- w_key_grad: float32 [2, 1024, 512], P(None, 'dp', 'tensor')
- w_value_grad: float32 [2, 1024, 512], P(None, 'dp', 'tensor')
- w_out_grad: float32 [2, 512, 1024], P(None, 'tensor', 'dp')
- w_up_grad: float32 [2, 1024, 4096], P(None, 'dp', 'tensor')
- w_down_grad: float32 [2, 4096, 1024], P(None, 'tensor', 'dp')
Inputs may be any that keep to these rules, and one draw needn't show every extreme that they name: `frame_counts`: frames of each clip; in every draw some clip has 8 frames and some clip has 1.
All inputs are finite; a program needn't handle non-finite values.
Results may differ from a plain program's by a relative error of at most 0.02.
The roundings to bfloat16 on the way count: a program that leaves them out, or rounds other values in their place, can miss the bound.
Values sent between devices are 32-bit elements; how exact they have to be, the bound alone decides.
A program may use at most 256 MiB of HBM per device.

v0:
```python
import jax
import jax.numpy as jnp
from jax import lax
from jax.sharding import PartitionSpec as P

HEAD_DIM = 64


EPS = 1e-05


def normalize(values):
    row_mean = jnp.mean(values, axis=-1, keepdims=True)
    centered = values - row_mean
    inv_std = lax.rsqrt(jnp.mean(centered * centered, axis=-1, keepdims=True) + EPS)
    return (centered * inv_std, inv_std)


def norm_back(grad_out, gain_row, normed, inv_std):
    scaled = grad_out * gain_row
    return inv_std * (
        scaled
        - jnp.mean(scaled, axis=-1, keepdims=True)
        - normed * jnp.mean(scaled * normed, axis=-1, keepdims=True)
    )


def project(values, weight):
    return jnp.einsum("srd,dc->src", values, weight, preferred_element_type=jnp.float32)


def times_transpose(grad_rows, weight):
    return lax.dot_general(
        grad_rows, weight, (((2,), (1,)), ((), ())), preferred_element_type=jnp.float32
    )


def contract_rows(left_side, right_side):
    return lax.dot_general(
        left_side, right_side, (((0, 1), (0, 1)), ((), ())), preferred_element_type=jnp.float32
    )


def gelu_slope(values):
    return (
        0.5 * (1.0 + lax.erf(values * 0.7071067811865476))
        + values * jnp.exp(-0.5 * values * values) * 0.3989422804014327
    )


def local(
    media,
    frame_counts,
    time_embed,
    latents,
    media_gain,
    media_bias,
    latent_gain,
    latent_bias,
    ff_gain,
    ff_bias,
    w_query,
    w_key,
    w_value,
    w_out,
    w_up,
    w_down,
    cotangent,
):
    samples, media_len, model_width = media.shape
    frames = time_embed.shape[0]
    patches = media_len // frames
    latent_rows = latents.shape[0]
    inner_width = w_query.shape[2]
    head_count = inner_width // HEAD_DIM
    depth_count = w_query.shape[0]
    key_count = media_len + latent_rows
    score_scale = HEAD_DIM ** (-0.5)
    media_in = (
        media.astype(jnp.float32).reshape(samples, frames, patches, model_width)
        + time_embed.astype(jnp.float32)[None, :, None, :]
    ).reshape(samples, media_len, model_width)
    media_normed, media_rstd = normalize(media_in)
    position = lax.broadcasted_iota(jnp.int32, (samples, key_count), 1)
    key_live = (position >= media_len) | (position // patches < frame_counts[:, None])
    key_mask = key_live[:, None, None, :]
    state = jnp.broadcast_to(latents.astype(jnp.float32)[None], (samples, latent_rows, model_width))

    def score_block(queries, kv_pair):
        query_heads = queries.reshape(samples, latent_rows, head_count, HEAD_DIM)
        key_heads = kv_pair[..., :inner_width].reshape(samples, key_count, head_count, HEAD_DIM)
        value_heads = kv_pair[..., inner_width:].reshape(samples, key_count, head_count, HEAD_DIM)
        scores = (
            jnp.einsum(
                "sqhd,skhd->shqk", query_heads, key_heads, preferred_element_type=jnp.float32
            )
            * score_scale
        )
        return (jnp.where(key_mask, scores, -1e30), query_heads, key_heads, value_heads)

    saved_list = []
    for depth in range(depth_count):
        w_pair = jnp.concatenate([w_key[depth], w_value[depth]], axis=1)
        media_x = (media_normed * media_gain[depth] + media_bias[depth]).astype(jnp.bfloat16)
        latent_normed, latent_rstd = normalize(state)
        latent_x = (latent_normed * latent_gain[depth] + latent_bias[depth]).astype(jnp.bfloat16)
        queries = project(latent_x, w_query[depth]).astype(jnp.bfloat16)
        kv_input = jnp.concatenate([media_x, latent_x], axis=1)
        kv_pair = project(kv_input, w_pair).astype(jnp.bfloat16)
        scores, query_heads, key_heads, value_heads = score_block(queries, kv_pair)
        row_max = jnp.max(scores, axis=-1, keepdims=True)
        exp_scores = jnp.exp(scores - row_max)
        row_total = jnp.sum(exp_scores, axis=-1, keepdims=True)
        attn_probs = exp_scores / row_total
        log_total = row_max + jnp.log(row_total)
        attended = jnp.einsum(
            "shqk,skhd->sqhd",
            attn_probs.astype(jnp.bfloat16),
            value_heads,
            preferred_element_type=jnp.float32,
        )
        attended = attended.astype(jnp.bfloat16).reshape(samples, latent_rows, inner_width)
        middle = state + lax.psum(project(attended, w_out[depth]), "tensor")
        ff_normed, ff_rstd = normalize(middle)
        ff_x = (ff_normed * ff_gain[depth] + ff_bias[depth]).astype(jnp.bfloat16)
        up_pre = project(ff_x, w_up[depth])
        hidden = jax.nn.gelu(up_pre, approximate=False).astype(jnp.bfloat16)
        ff_out = lax.psum(project(hidden, w_down[depth]), "tensor")
        saved_list.append(
            (
                latent_normed,
                latent_rstd,
                latent_x,
                queries,
                kv_input,
                kv_pair,
                log_total,
                attended,
                ff_normed,
                ff_rstd,
                ff_x,
                up_pre,
                hidden,
                w_pair,
            )
        )
        state = middle + ff_out
    upstream = cotangent
    media_total = jnp.zeros((samples, media_len, model_width), jnp.float32)
    summed = []
    gain_parts = []
    for depth in reversed(range(depth_count)):
        (
            latent_normed,
            latent_rstd,
            latent_x,
            queries,
            kv_input,
            kv_pair,
            log_total,
            attended,
            ff_normed,
            ff_rstd,
            ff_x,
            up_pre,
            hidden,
            w_pair,
        ) = saved_list[depth]
        upstream_low = upstream.astype(jnp.bfloat16)
        grad_down = contract_rows(hidden, upstream_low)
        grad_hidden = times_transpose(upstream_low, w_down[depth])
        grad_pre = (grad_hidden * gelu_slope(up_pre)).astype(jnp.bfloat16)
        grad_up = contract_rows(ff_x, grad_pre)
        grad_ffx = lax.psum(times_transpose(grad_pre, w_up[depth]), "tensor")
        ff_gain_part = jnp.sum(grad_ffx * ff_normed, axis=(0, 1))
        ff_bias_part = jnp.sum(grad_ffx, axis=(0, 1))
        grad_middle = upstream + norm_back(grad_ffx, ff_gain[depth], ff_normed, ff_rstd)
        middle_low = grad_middle.astype(jnp.bfloat16)
        grad_outw = contract_rows(attended, middle_low)
        grad_att = times_transpose(middle_low, w_out[depth]).astype(jnp.bfloat16)
        grad_heads = grad_att.reshape(samples, latent_rows, head_count, HEAD_DIM)
        scores, query_heads, key_heads, value_heads = score_block(queries, kv_pair)
        attn_probs = jnp.exp(scores - log_total)
        grad_probs = jnp.einsum(
            "sqhd,skhd->shqk", grad_heads, value_heads, preferred_element_type=jnp.float32
        )
        row_delta = jnp.sum(attn_probs * grad_probs, axis=-1, keepdims=True)
        grad_scores = (attn_probs * (grad_probs - row_delta)).astype(jnp.bfloat16)
        grad_query = (
            (
                jnp.einsum(
                    "shqk,skhd->sqhd", grad_scores, key_heads, preferred_element_type=jnp.float32
                )
                * score_scale
            )
            .astype(jnp.bfloat16)
            .reshape(samples, latent_rows, inner_width)
        )
        grad_key = (
            (
                jnp.einsum(
                    "shqk,sqhd->skhd", grad_scores, query_heads, preferred_element_type=jnp.float32
                )
                * score_scale
            )
            .astype(jnp.bfloat16)
            .reshape(samples, key_count, inner_width)
        )
        grad_value = jnp.einsum(
            "shqk,sqhd->skhd",
            attn_probs.astype(jnp.bfloat16),
            grad_heads,
            preferred_element_type=jnp.float32,
        ).astype(jnp.bfloat16)
        grad_pair = jnp.concatenate(
            [grad_key, grad_value.reshape(samples, key_count, inner_width)], axis=-1
        )
        grad_queryw = contract_rows(latent_x, grad_query)
        grad_pairw = contract_rows(kv_input, grad_pair)
        grad_rows = times_transpose(grad_pair, w_pair)
        grad_latx = lax.psum(
            times_transpose(grad_query, w_query[depth]) + grad_rows[:, media_len:], "tensor"
        )
        grad_media = grad_rows[:, :media_len]
        media_gain_part = jnp.sum(grad_media * media_normed, axis=(0, 1))
        media_bias_part = jnp.sum(grad_media, axis=(0, 1))
        media_total = media_total + norm_back(
            grad_media, media_gain[depth], media_normed, media_rstd
        )
        latent_gain_part = jnp.sum(grad_latx * latent_normed, axis=(0, 1))
        latent_bias_part = jnp.sum(grad_latx, axis=(0, 1))
        upstream = grad_middle + norm_back(
            grad_latx, latent_gain[depth], latent_normed, latent_rstd
        )
        gain_parts.append(
            (
                media_gain_part,
                media_bias_part,
                latent_gain_part,
                latent_bias_part,
                ff_gain_part,
                ff_bias_part,
            )
        )
        layer_grads = (
            grad_queryw,
            grad_pairw[:, :inner_width],
            grad_pairw[:, inner_width:],
            grad_outw,
            grad_up,
            grad_down,
        )
        summed.append(layer_grads)
    ordered = summed[::-1]
    stacked = tuple(
        (jnp.stack([entry_tuple[member] for entry_tuple in ordered]) for member in range(6))
    )
    stacked = (
        lax.psum_scatter(stacked[0], "dp", scatter_dimension=1, tiled=True),
        lax.psum_scatter(stacked[1], "dp", scatter_dimension=1, tiled=True),
        lax.psum_scatter(stacked[2], "dp", scatter_dimension=1, tiled=True),
        lax.psum_scatter(stacked[3], "dp", scatter_dimension=2, tiled=True),
        lax.psum_scatter(stacked[4], "dp", scatter_dimension=1, tiled=True),
        lax.psum_scatter(stacked[5], "dp", scatter_dimension=2, tiled=True),
    )
    gain_order = gain_parts[::-1]
    gain_stacks = [
        jnp.stack([entry_tuple[member] for entry_tuple in gain_order]) for member in range(6)
    ]
    tensor_share = 1.0 / lax.axis_size("tensor")
    time_part = jnp.sum(media_total.reshape(samples, frames, patches, model_width), axis=(0, 2))
    latent_part = jnp.sum(upstream, axis=0) * tensor_share
    small_sums = lax.psum(
        (
            gain_stacks[0],
            gain_stacks[1],
            gain_stacks[2] * tensor_share,
            gain_stacks[3] * tensor_share,
            gain_stacks[4] * tensor_share,
            gain_stacks[5] * tensor_share,
            time_part,
            latent_part,
        ),
        ("dp", "tensor"),
    )
    media_grad = lax.psum_scatter(media_total, "tensor", scatter_dimension=2, tiled=True).astype(
        jnp.bfloat16
    )
    return (
        state,
        media_grad,
        small_sums[6],
        small_sums[7],
        small_sums[0],
        small_sums[1],
        small_sums[2],
        small_sums[3],
        small_sums[4],
        small_sums[5],
        stacked[0],
        stacked[1],
        stacked[2],
        stacked[3],
        stacked[4],
        stacked[5],
    )


def solution(mesh):
    in_specs = (
        P("dp", None, None),
        P("dp"),
        P(),
        P(),
        P(),
        P(),
        P(),
        P(),
        P(),
        P(),
        P(None, None, "tensor"),
        P(None, None, "tensor"),
        P(None, None, "tensor"),
        P(None, "tensor", None),
        P(None, None, "tensor"),
        P(None, "tensor", None),
        P("dp", None, None),
    )
    out_specs = (
        P("dp", None, None),
        P("dp", None, "tensor"),
        P(),
        P(),
        P(),
        P(),
        P(),
        P(),
        P(),
        P(),
        P(None, "dp", "tensor"),
        P(None, "dp", "tensor"),
        P(None, "dp", "tensor"),
        P(None, "tensor", "dp"),
        P(None, "dp", "tensor"),
        P(None, "tensor", "dp"),
    )
    return jax.shard_map(local, mesh=mesh, in_specs=in_specs, out_specs=out_specs, check_vma=False)
```

profile of v0, /device:TPU:0, one launch (start us, length us, event | category | flops | bytes accessed | tf_op | source)
XLA Modules:
  0.0 1517.2 jit_solution(5393629182638126152)
XLA Ops:
  14.8 10.3 fusion.1
  25.2 5.0 multiply_reduce_fusion.4
  31.4 11.5 add_convert_fusion
  42.9 8.2 fusion.9
  66.5 34.4 %all-reduce.12.cloned.1.call-done = f32[3,64,1024]{2,1,0:T(8,128)} async-done(((f32[3,64,1024]{2,1,0:T(8,128)}), f32[3,64,1024]{2,1,0:T(8,128)}) %all-reduce.12.cloned.1.call-update) | async-done | bytes 786448 | tf_op jit(solution)/shard_map/psum | solution.py:123
  103.7 3.0 fusion.136
  111.7 34.8 %all-reduce.14.cloned.1.call-done = f32[3,64,1024]{2,1,0:T(8,128)} async-done(((f32[3,64,1024]{2,1,0:T(8,128)}), f32[3,64,1024]{2,1,0:T(8,128)}) %all-reduce.14.cloned.1.call-update) | async-done | bytes 786448 | tf_op jit(solution)/shard_map/psum | solution.py:128
  150.2 8.1 fusion.10
  160.6 3.8 copy.90
  165.3 3.8 copy.89
  177.1 34.4 %all-reduce.16.cloned.1.call-done = f32[3,64,1024]{2,1,0:T(8,128)} async-done(((f32[3,64,1024]{2,1,0:T(8,128)}), f32[3,64,1024]{2,1,0:T(8,128)}) %all-reduce.16.cloned.1.call-update) | async-done | bytes 786448 | tf_op jit(solution)/shard_map/psum | solution.py:123
  213.9 3.9 fusion.137
  222.9 34.1 %all-reduce.18.cloned.1.call-done = f32[3,64,1024]{2,1,0:T(8,128)} async-done(((f32[3,64,1024]{2,1,0:T(8,128)}), f32[3,64,1024]{2,1,0:T(8,128)}) %all-reduce.18.cloned.1.call-update) | async-done | bytes 786448 | tf_op jit(solution)/shard_map/psum | solution.py:174
  257.0 2.4 multiply_reduce_fusion.7
  264.6 3.5 multiply_reduce_fusion.6
  273.3 3.8 copy.96
  277.0 3.7 copy.97
  280.7 14.2 fusion.36
  295.0 2.3 convolution_add_fusion.1
  298.2 33.9 %all-reduce.20.cloned.1.call-done = f32[3,64,1024]{2,1,0:T(8,128)} async-done(((f32[3,64,1024]{2,1,0:T(8,128)}), f32[3,64,1024]{2,1,0:T(8,128)}) %all-reduce.20.cloned.1.call-update) | async-done | bytes 786448 | tf_op jit(solution)/shard_map/psum | solution.py:221
  332.1 2.4 multiply_reduce_fusion.9
  337.4 2.7 fusion.62
  342.7 2.9 fusion.87
  346.3 3.0 fusion.21
  349.4 28.1 %all-reduce.22.cloned.1.call-done = f32[3,64,1024]{2,1,0:T(8,128)} async-done(((f32[3,64,1024]{2,1,0:T(8,128)}), f32[3,64,1024]{2,1,0:T(8,128)}) %all-reduce.22.cloned.1.call-update) | async-done | bytes 786448 | tf_op jit(solution)/shard_map/psum | solution.py:174
  377.5 2.5 multiply_reduce_fusion.8
  384.6 2.3 multiply_reduce_fusion.5
  391.7 2.4 copy.102
  396.3 13.7 fusion.35
  410.0 24.2 %multiply_reduce_fusion = (f32[1024]{0:T(1024)S(1)}, f32[3,2048]{1,0:T(4,128)S(1)}, f32[3,2048]{1,0:T(4,128)S(1)}, f32[1024]{0:T(1024)S(1)}, f32[1024]{0:T(1024)...) fusion(bf16[3,2048,1024]{2,1,0:T(8,128)(2,1)} %param.17, f32[3,2112,1024]{2,1,0:T(8,128)} %fusion.36, ...), kind=kLoop, calls=%fused_computation.1 | loop fusion | flops 113217536 | bytes 71475200 | tf_op jit(solution)/shard_map/reduce_sum | solution.py:225
  434.1 2.3 convolution_add_fusion
  436.6 36.3 %fusion.150 = (f32[2048,1024]{1,0:T(8,128)}, f32[3,2048,1024]{2,1,0:T(8,128)}) fusion(f32[3,2048]{1,0:T(4,128)S(1)} %broadcast_multiply_fusion.1, f32[3,2048]{1,0:T(4,128)S(1)} %broadcast_multiply_fusion.2, f32[1024]{0:T(1024)S(1)} %bitcast.265, f32[3,2112,1024]{2,1,0:T(8,128)} %fusion.35, f32[3,2048]{1,0:T(4,128)S(1)} %broadcast_multiply_fusion.3, ...), kind=kLoop, calls=%fused_computation.295 | loop fusion | flops 92274688 | bytes 105013248 | tf_op jit(solution)/shard_map/reduce_sum | solution.py:271
  478.7 4.8 bitcast_reduce_fusion
  488.7 2.3 pad_maximum_fusion.29
  491.1 11.3 fusion.52
  502.6 9.6 fusion.51
  518.7 4.1 pad_maximum_fusion.3
  525.9 4.1 pad_maximum_fusion.2
  532.0 130.9 %reduce-scatter.8.cloned.1.call-done = f32[3,2048,256]{2,1,0:T(8,128)} async-done(((f32[3,2048,1024]{2,1,0:T(8,128)}), f32[3,2048,256]{2,1,0:T(8,128)}) %reduce-scatter.8.cloned.1.call-update) | async-done | bytes 6291472 | tf_op jit(solution)/shard_map/reduce_scatter | solution.py:286
  662.9 4.8 convert_element_type.181
  667.7 127.8 %all-reduce.26.cloned.1.call-done = (f32[8,1024]{1,0:T(8,128)}, f32[2,1024]{1,0:T(2,128)}, f32[2,1024]{1,0:T(2,128)}, f32[2,1024]{1,0:T(2,128)}, f32[2,1024]{1,0...) async-done(((f32[8,1024]{1,0:T(8,128)}, f32[2,1024]{1,0:T(2,128)}, f32[2,1024]{1,0:T(2,128)}, f32[2,1024]{1,0:T(2,128)}, f32[2,1024]{1,0:T(2,128)}, ...) | async-done | bytes 81936 | tf_op jit(solution)/shard_map/psum | solution.py:273
  795.4 132.1 %all-reduce.24.cloned.1.call-done = f32[64,1024]{1,0:T(8,128)} async-done(((f32[64,1024]{1,0:T(8,128)}), f32[64,1024]{1,0:T(8,128)}) %all-reduce.24.cloned.1.call-update) | async-done | bytes 262160 | tf_op jit(solution)/shard_map/psum | solution.py:273
  927.5 66.9 %reduce-scatter.16.cloned.1.call-done = f32[2,128,128]{2,1,0:T(8,128)} async-done(((f32[2,128,1024]{2,1,0:T(8,128)}), f32[2,128,128]{2,1,0:T(8,128)}) %reduce-scatter.16.cloned.1.call-update) | async-done | bytes 131088 | tf_op jit(solution)/shard_map/reduce_scatter | solution.py:262
  994.4 66.6 %reduce-scatter.14.cloned.1.call-done = f32[2,128,128]{2,1,0:T(8,128)} async-done(((f32[2,1024,128]{2,1,0:T(8,128)}), f32[2,128,128]{2,1,0:T(8,128)}) %reduce-scatter.14.cloned.1.call-update) | async-done | bytes 131088 | tf_op jit(solution)/shard_map/reduce_scatter | solution.py:261
  1061.1 66.5 %reduce-scatter.12.cloned.1.call-done = f32[2,128,128]{2,1,0:T(8,128)} async-done(((f32[2,1024,128]{2,1,0:T(8,128)}), f32[2,128,128]{2,1,0:T(8,128)}) %reduce-scatter.12.cloned.1.call-update) | async-done | bytes 131088 | tf_op jit(solution)/shard_map/reduce_scatter | solution.py:260
  1127.6 66.7 %reduce-scatter.10.cloned.1.call-done = f32[2,128,128]{2,1,0:T(8,128)} async-done(((f32[2,1024,128]{2,1,0:T(8,128)}), f32[2,128,128]{2,1,0:T(8,128)}) %reduce-scatter.10.cloned.1.call-update) | async-done | bytes 131088 | tf_op jit(solution)/shard_map/reduce_scatter | solution.py:259
  1194.3 152.5 %reduce-scatter.20.cloned.1.call-done = f32[2,1024,128]{2,1,0:T(8,128)} async-done(((f32[2,1024,1024]{2,1,0:T(8,128)}), f32[2,1024,128]{2,1,0:T(8,128)}) %reduce-scatter.20.cloned.1.call-update) | async-done | bytes 1048592 | tf_op jit(solution)/shard_map/reduce_scatter | solution.py:264
  1346.9 152.5 %reduce-scatter.18.cloned.1.call-done = f32[2,128,1024]{2,1,0:T(8,128)} async-done(((f32[2,1024,1024]{2,1,0:T(8,128)}), f32[2,128,1024]{2,1,0:T(8,128)}) %reduce-scatter.18.cloned.1.call-update) | async-done | bytes 1048592 | tf_op jit(solution)/shard_map/reduce_scatter | solution.py:263
  (400 shorter events, 116.0 us)
Async XLA Ops:
  7.2 93.8 %all-reduce.12.cloned.1.call-start = ((), (), s32[]{:S(2)}) async-start(), calls=%async_computation.7 | async-start | bytes 1572864 | tf_op jit(solution)/shard_map/psum | solution.py:123
  8.2 45.7 %copy-start.3 = (f32[64,1024]{1,0:T(8,128)}, f32[64,1024]{1,0:T(8,128)S(1)}, u32[]{:S(2)}) copy-start(f32[64,1024]{1,0:T(8,128)S(1)} %convert_element_type.138) | copy-start | bytes 786436
  9.9 21.3 %copy-start.114 = (f32[64]{0:T(128)}, f32[64]{0:T(128)S(1)}, u32[]{:S(2)}) copy-start(f32[64]{0:T(128)S(1)} %broadcast_multiply_fusion.17) | copy-start | bytes 772
  10.1 43.8 %copy-start.90 = (f32[3,64]{1,0:T(4,128)}, f32[3,64]{1,0:T(4,128)S(1)}, u32[]{:S(2)}) copy-start(f32[3,64]{1,0:T(4,128)S(1)} %add_rsqrt_fusion.4) | copy-start | bytes 2308
  11.5 42.4 %copy-start.66 = (f32[1,1024]{1,0:T(1,128)}, f32[1,1024]{1,0:T(1,128)S(1)}, u32[]{:S(2)}) copy-start(f32[1,1024]{1,0:T(1,128)S(1)} %get-tuple-element.87) | copy-start | bytes 12292
  12.8 41.0 %copy-start.98 = (f32[1,1024]{1,0:T(1,128)}, f32[1,1024]{1,0:T(1,128)S(1)}, u32[]{:S(2)}) copy-start(f32[1,1024]{1,0:T(1,128)S(1)} %get-tuple-element.89) | copy-start | bytes 12292
  12.8 12.3 slice-start
  14.8 16.6 %copy-start = (f32[8,256,1024]{2,1,0:T(8,128)}, f32[8,256,1024]{2,1,0:T(8,128)S(1)}, u32[]{:S(2)}) copy-start(f32[8,256,1024]{2,1,0:T(8,128)S(1)} %add.225) | copy-start | bytes 25165828
  30.2 12.7 copy-start.54
  30.2 12.6 copy-start.76
  30.2 12.6 copy-start.78
  31.2 11.7 copy-start.40
  31.2 11.7 copy-start.41
  31.4 11.5 copy-start.60
  62.1 44.6 %copy-start.62 = (bf16[3,2,64,64]{3,2,1,0:T(8,128)(2,1)}, bf16[3,2,64,64]{3,2,1,0:T(8,128)(2,1)S(1)}, u32[]{:S(2)}) copy-start(bf16[3,2,64,64]{3,2,1,0:T(8,128)(2,1)S(1)} %fusion.68) | copy-start | bytes 147460
  63.5 83.0 %all-reduce.14.cloned.1.call-start = ((), (), s32[]{:S(2)}) async-start(), calls=%async_computation.8 | async-start | bytes 1572864 | tf_op jit(solution)/shard_map/psum | solution.py:128
  65.1 314.8 %copy-start.69 = (f32[1,1024]{1,0:T(1,128)}, f32[1,1024]{1,0:T(1,128)S(1)}, u32[]{:S(2)}) copy-start(f32[1,1024]{1,0:T(1,128)S(1)} %get-tuple-element.79) | copy-start | bytes 12292
  110.2 38.9 %copy-start.73 = (f32[1,1024]{1,0:T(1,128)S(1)}, f32[1,1024]{1,0:T(1,128)}, u32[]{:S(2)}) copy-start(f32[1,1024]{1,0:T(1,128)} %get-tuple-element.86) | copy-start | bytes 12292
  110.2 38.9 %copy-start.106 = (f32[1,1024]{1,0:T(1,128)S(1)}, f32[1,1024]{1,0:T(1,128)}, u32[]{:S(2)}) copy-start(f32[1,1024]{1,0:T(1,128)} %get-tuple-element.88) | copy-start | bytes 12292
  111.7 99.8 %all-reduce.16.cloned.1.call-start = ((), (), s32[]{:S(2)}) async-start(), calls=%async_computation.9 | async-start | bytes 1572864 | tf_op jit(solution)/shard_map/psum | solution.py:123
  174.8 39.1 %copy-start.71 = (f32[1,1024]{1,0:T(1,128)S(1)}, f32[1,1024]{1,0:T(1,128)}, u32[]{:S(2)}) copy-start(f32[1,1024]{1,0:T(1,128)} %get-tuple-element.78) | copy-start | bytes 12292
  176.7 80.3 %all-reduce.18.cloned.1.call-start = ((), (), s32[]{:S(2)}) async-start(), calls=%async_computation.10 | async-start | bytes 1572864 | tf_op jit(solution)/shard_map/psum | solution.py:174
  213.1 46.3 %copy-start.80 = (f32[3,64]{1,0:T(4,128)}, f32[3,64]{1,0:T(4,128)S(1)}, u32[]{:S(2)}) copy-start(f32[3,64]{1,0:T(4,128)S(1)} %broadcast_multiply_fusion.14) | copy-start | bytes 2308
  222.1 110.0 %all-reduce.20.cloned.1.call-start = ((), (), s32[]{:S(2)}) async-start(), calls=%async_computation.11 | async-start | bytes 1572864 | tf_op jit(solution)/shard_map/psum | solution.py:221
  273.2 21.7 %copy-start.44 = (bf16[3,2,64,64]{3,2,1,0:T(8,128)(2,1)}, bf16[3,2,64,64]{3,2,1,0:T(8,128)(2,1)S(1)}, u32[]{:S(2)}) copy-start(bf16[3,2,64,64]{3,2,1,0:T(8,128)(2,1)S(1)} %fusion.65) | copy-start | bytes 147460
  280.7 14.2 copy-start.37
  280.7 51.4 %copy-start.74 = (f32[1,1024]{1,0:T(1,128)S(1)}, f32[1,1024]{1,0:T(1,128)}, u32[]{:S(2)}) copy-start(f32[1,1024]{1,0:T(1,128)} %get-tuple-element.86) | copy-start | bytes 12292
  280.7 51.4 %copy-start.83 = (f32[3,64]{1,0:T(4,128)S(1)}, f32[3,64]{1,0:T(4,128)}, u32[]{:S(2)}) copy-start(f32[3,64]{1,0:T(4,128)} %copy-done.82) | copy-start | bytes 2308
  297.3 80.1 %all-reduce.22.cloned.1.call-start = ((), (), s32[]{:S(2)}) async-start(), calls=%async_computation.12 | async-start | bytes 1572864 | tf_op jit(solution)/shard_map/psum | solution.py:174
  342.6 34.9 %copy-start.85 = (f32[3,64]{1,0:T(4,128)S(1)}, f32[3,64]{1,0:T(4,128)}, u32[]{:S(2)}) copy-start(f32[3,64]{1,0:T(4,128)} %copy-done.84) | copy-start | bytes 2308
  342.6 34.9 %copy-start.94 = (f32[3,64]{1,0:T(4,128)S(1)}, f32[3,64]{1,0:T(4,128)}, u32[]{:S(2)}) copy-start(f32[3,64]{1,0:T(4,128)} %copy-done.93) | copy-start | bytes 2308
  342.6 140.8 %all-reduce.28.cloned.1.call-start = ((), (), s32[]{:S(2)}) async-start(), calls=%async_computation.22 | async-start | bytes 3145728 | tf_op jit(solution)/shard_map/psum | solution.py:128
  396.2 13.7 copy-start.47
  396.2 13.7 copy-start.55
  396.2 13.7 copy-start.77
  396.2 13.7 copy-start.79
  410.0 24.2 %copy-start.38 = (bf16[2,1024,128]{2,1,0:T(8,128)(2,1)S(1)}, bf16[2,1024,128]{2,1,0:T(8,128)(2,1)}, u32[]{:S(2)}) copy-start(bf16[2,1024,128]{2,1,0:T(8,128)(2,1)} %param.27) | copy-start | bytes 1572868
  436.5 226.4 %reduce-scatter.8.cloned.1.call-start = ((), (), s32[]{:S(2)}) async-start(), calls=%async_computation.13 | async-start | bytes 31457280 | tf_op jit(solution)/shard_map/reduce_scatter | solution.py:286
  473.0 322.4 %all-reduce.26.cloned.1.call-start = ((), (), s32[]{:S(2)}) async-start(), calls=%async_computation.21 | async-start | bytes 163840 | tf_op jit(solution)/shard_map/psum | solution.py:273
  487.8 439.7 %all-reduce.24.cloned.1.call-start = ((), (), s32[]{:S(2)}) async-start(), calls=%async_computation.14 | async-start | bytes 524288 | tf_op jit(solution)/shard_map/psum | solution.py:273
  488.6 505.8 %reduce-scatter.16.cloned.1.call-start = ((), (), s32[]{:S(2)}) async-start(), calls=%async_computation.18 | async-start | bytes 1179648 | tf_op jit(solution)/shard_map/reduce_scatter | solution.py:262
  491.0 11.5 copy-start.61
  491.1 570.0 %reduce-scatter.14.cloned.1.call-start = ((), (), s32[]{:S(2)}) async-start(), calls=%async_computation.17 | async-start | bytes 1179648 | tf_op jit(solution)/shard_map/reduce_scatter | solution.py:261
  491.1 11.5 copy-start.22
  513.4 614.1 %reduce-scatter.12.cloned.1.call-start = ((), (), s32[]{:S(2)}) async-start(), calls=%async_computation.16 | async-start | bytes 1179648 | tf_op jit(solution)/shard_map/reduce_scatter | solution.py:260
  514.6 679.8 %reduce-scatter.10.cloned.1.call-start = ((), (), s32[]{:S(2)}) async-start(), calls=%async_computation.15 | async-start | bytes 1179648 | tf_op jit(solution)/shard_map/reduce_scatter | solution.py:259
  516.7 830.1 %reduce-scatter.20.cloned.1.call-start = ((), (), s32[]{:S(2)}) async-start(), calls=%async_computation.20 | async-start | bytes 9437184 | tf_op jit(solution)/shard_map/reduce_scatter | solution.py:264
  523.0 976.4 %reduce-scatter.18.cloned.1.call-start = ((), (), s32[]{:S(2)}) async-start(), calls=%async_computation.19 | async-start | bytes 9437184 | tf_op jit(solution)/shard_map/reduce_scatter | solution.py:263
  (94 other events, 322.7 us)
Sparse Core Ops, SparseCore 0:
  63.6 37.2 all-reduce.11
  111.8 34.6 all-reduce.13
  176.8 34.6 all-reduce.15
  222.2 34.6 all-reduce.17
  297.4 34.6 all-reduce.19
  342.7 34.6 all-reduce.21
  436.7 43.1 all-reduce.27
  482.4 180.4 reduce-scatter.7
  671.6 123.7 all-reduce.25
  801.3 126.1 all-reduce.23
  931.5 62.8 reduce-scatter.15
  998.6 62.3 reduce-scatter.13
  1065.0 62.4 reduce-scatter.11
  1131.8 62.4 reduce-scatter.9
  1198.4 148.4 reduce-scatter.19
  1351.4 148.0 reduce-scatter.17
where the time goes:
time: 1530 us; the launch traced here: 1520 us
  waiting for transfers between devices  1160 us (76%)
  other arithmetic  151 us (10%)
  matrix products  120 us (8%)
  local copies, waits for them, and re-layouts  66.7 us (4%)
  between operations  15.9 us (1%)
    psum x2, waiting for transfers between devices, local(): lax.psum((gain_stacks[0], gain_stacks[1], gain_stacks[2] * tensor_share,...  260 us
    reduce_scatter x1, waiting for transfers between devices, local(): lax.psum_scatter(stacked[5], 'dp', scatter_dimension=2, tiled=True)  153 us
    reduce_scatter x1, waiting for transfers between devices, local(): lax.psum_scatter(stacked[4], 'dp', scatter_dimension=1, tiled=True)  153 us
    reduce_scatter x1, waiting for transfers between devices, local(): lax.psum_scatter(media_total, 'tensor', scatter_dimension=2, tiled=True)  131 us
    psum x2, waiting for transfers between devices, local(): middle = state + lax.psum(project(attended, w_out[depth]), 'tensor')  68.8 us
    reduce_scatter x1, waiting for transfers between devices, local(): lax.psum_scatter(stacked[3], 'dp', scatter_dimension=2, tiled=True)  66.9 us
    reduce_scatter x1, waiting for transfers between devices, local(): lax.psum_scatter(stacked[0], 'dp', scatter_dimension=1, tiled=True)  66.7 us
    reduce_scatter x1, waiting for transfers between devices, local(): lax.psum_scatter(stacked[2], 'dp', scatter_dimension=1, tiled=True)  66.6 us
  transfers between devices with their start and end apart: 16, of which 15 were waited for; matrix products, arithmetic and copies ran while one was open for 7% of the time, Pallas kernels for 0%

commit v1 on v0

v1 whole, which is shorter than its diff:
```python
import jax
import jax.numpy as jnp
from jax import lax
from jax.sharding import PartitionSpec as P

HEAD_DIM = 64
EPS = 1e-05
F32 = jnp.float32
BF16 = jnp.bfloat16


def normalize(values):
    row_mean = jnp.mean(values, axis=-1, keepdims=True)
    centered = values - row_mean
    inv_std = lax.rsqrt(jnp.mean(centered * centered, axis=-1, keepdims=True) + EPS)
    return (centered * inv_std, inv_std)


def norm_back(grad_out, gain_row, normed, inv_std):
    scaled = grad_out * gain_row
    return inv_std * (
        scaled
        - jnp.mean(scaled, axis=-1, keepdims=True)
        - normed * jnp.mean(scaled * normed, axis=-1, keepdims=True)
    )


def mm(left_side, right_side):
    return jnp.dot(left_side, right_side, preferred_element_type=F32)


def mm_bt(left_side, right_side):
    return lax.dot_general(left_side, right_side, (((1,), (1,)), ((), ())), preferred_element_type=F32)


def mm_at(left_side, right_side):
    return lax.dot_general(left_side, right_side, (((0,), (0,)), ((), ())), preferred_element_type=F32)


def gelu_slope(values):
    return (
        0.5 * (1.0 + lax.erf(values * 0.7071067811865476))
        + values * jnp.exp(-0.5 * values * values) * 0.3989422804014327
    )


class Links:

    def __init__(self, zero):
        self.zero = zero
        self.tensor_size = lax.axis_size("tensor")
        self.dp_size = lax.axis_size("dp")
        self.groups = self.tensor_size // 2
        self.planes = self.dp_size // 2
        tensor_at = lax.axis_index("tensor")
        dp_at = lax.axis_index("dp")
        self.core = lax.rem(tensor_at, 2)
        self.group = lax.div(tensor_at, 2)
        self.side = lax.rem(dp_at, 2)
        self.plane = lax.div(dp_at, 2)

    def arrive(self, value):
        return value + self.zero

    def core_swap(self, value):
        return lax.ppermute(value, "tensor", [(i, i ^ 1) for i in range(self.tensor_size)])

    def group_turn(self, value, turn):
        size = self.tensor_size
        return lax.ppermute(value, "tensor", [(i, (i + 2 * turn) % size) for i in range(size)])

    def side_swap(self, value):
        return lax.ppermute(value, "dp", [(i, i ^ 1) for i in range(self.dp_size)])

    def cut(self, value, index):
        half = value.shape[0] // 2
        return lax.dynamic_slice_in_dim(value, index * half, half, 0)

    def join(self, mine, other, index):
        first = index == 0
        return jnp.concatenate([jnp.where(first, mine, other), jnp.where(first, other, mine)], axis=0)

    def group_sum(self, value):
        if self.groups == 2:
            return value + self.group_turn(value, 1)
        turned = jnp.stack([value] + [self.group_turn(value, k) for k in range(1, self.groups)])
        total = None
        for source in range(self.groups):
            slot = lax.rem(self.group - source + self.groups, self.groups)
            term = lax.dynamic_index_in_dim(turned, slot, 0, keepdims=False)
            total = term if total is None else total + term
        return total

    def core_sum(self, value):
        return value + self.core_swap(value)

    def tensor_sum(self, value):
        mine = self.cut(value, self.core) + self.core_swap(self.cut(value, 1 - self.core))
        mine = self.group_sum(mine)
        return self.join(mine, self.core_swap(mine), self.core)

    def dp_sum(self, value):
        step = 1
        while step < self.dp_size:
            value = value + lax.ppermute(value, "dp", [(i, i ^ step) for i in range(self.dp_size)])
            step *= 2
        return value

    def line_scatter(self, partial):
        planes = self.planes
        chain = {}
        for way in (1, -1):
            place = self.plane if way == 1 else planes - 1 - self.plane
            arrived = None
            for step in range(1, planes):
                index = jnp.minimum(planes - step + place, planes - 1)
                if way == -1:
                    index = planes - 1 - index
                share = partial(index)
                if arrived is not None:
                    share = share + arrived
                pairs = []
                for at in range(step):
                    source, target = at, at + 1
                    if way == -1:
                        source, target = planes - 1 - source, planes - 1 - target
                    pairs += [(2 * source + s, 2 * target + s) for s in range(2)]
                arrived = lax.ppermute(share, "dp", pairs)
            chain[way] = arrived
        return partial(self.plane) + chain[1] + chain[-1]

    def side_rows(self, value):
        value = value.astype(F32)
        return jnp.concatenate([value.astype(BF16), self.arrive(self.side_swap(value)).astype(BF16)], axis=0)

    def side_columns(self, value):
        rows, width = value.shape
        split = value.astype(F32).reshape(rows, self.planes, 2, width // self.dp_size)
        mine = lax.dynamic_index_in_dim(split, self.side, 2, keepdims=False)
        theirs = lax.dynamic_index_in_dim(split, 1 - self.side, 2, keepdims=False)
        half = self.side_swap(self.cut(theirs, self.core))
        other = self.arrive(self.join(half, self.core_swap(half), self.core))
        both = jnp.concatenate([mine.astype(BF16), other.astype(BF16)], axis=0)
        return jnp.transpose(both, (1, 0, 2))


def local(
    media,
    frame_counts,
    time_embed,
    latents,
    media_gain,
    media_bias,
    latent_gain,
    latent_bias,
    ff_gain,
    ff_bias,
    w_query,
    w_key,
    w_value,
    w_out,
    w_up,
    w_down,
    cotangent,
):
    links = Links(jnp.where(frame_counts[0] > 1000000, 1.0, 0.0).astype(F32))
    samples, media_len, width = media.shape
    frames = time_embed.shape[0]
    patches = media_len // frames
    latent_rows = latents.shape[0]
    own = w_query.shape[2]
    layers = w_query.shape[0]
    wide = own * links.groups
    heads = wide // HEAD_DIM
    key_count = media_len + latent_rows
    score_scale = HEAD_DIM ** (-0.5)
    rows = samples * latent_rows

    def gather(weight):
        mine = weight.astype(F32)
        half = links.cut(mine, links.side)
        parts = [weight]
        for turn in range(1, links.groups):
            arrived = links.group_turn(half, turn)
            parts.append(links.arrive(links.join(arrived, links.side_swap(arrived), links.side)).astype(BF16))
        return parts

    query4, key4, value4, out4 = [], [], [], []
    for depth in range(layers):
        parts = gather(jnp.concatenate([w_key[depth], w_value[depth]], axis=1))
        key4.append(jnp.concatenate([p[:, :own] for p in parts], axis=1))
        value4.append(jnp.concatenate([p[:, own:] for p in parts], axis=1))
        parts = gather(jnp.concatenate([w_query[depth], w_out[depth].T], axis=1))
        query4.append(jnp.concatenate([p[:, :own] for p in parts], axis=1))
        out4.append(jnp.concatenate([p[:, own:] for p in parts], axis=1))
    pair4 = [jnp.concatenate([key4[l], value4[l]], axis=1) for l in range(layers)]

    media_in = (
        media.astype(F32).reshape(samples, frames, patches, width)
        + time_embed.astype(F32)[None, :, None, :]
    ).reshape(samples * media_len, width)
    media_normed, media_rstd = normalize(media_in)
    position = lax.broadcasted_iota(jnp.int32, (samples, key_count), 1)
    key_live = (position >= media_len) | (position // patches < frame_counts[:, None])
    key_mask = key_live[:, None, None, :]
    state = jnp.broadcast_to(latents.astype(F32)[None], (samples, latent_rows, width)).reshape(rows, width)

    def heads_of(value):
        return value.reshape(samples, -1, heads, HEAD_DIM)

    def score_block(queries, keys):
        scores = jnp.einsum("sqhd,skhd->shqk", heads_of(queries), keys, preferred_element_type=F32)
        return jnp.where(key_mask, scores * score_scale, -1e30)

    media_x = [(media_normed * media_gain[l] + media_bias[l]).astype(BF16) for l in range(layers)]
    media_pair = [mm(media_x[l], pair4[l]).astype(BF16) for l in range(layers)]

    saved = []
    for depth in range(layers):
        latent_normed, latent_rstd = normalize(state)
        latent_x = (latent_normed * latent_gain[depth] + latent_bias[depth]).astype(BF16)
        queries = mm(latent_x, query4[depth]).astype(BF16)
        latent_pair = mm(latent_x, pair4[depth]).astype(BF16)
        pair = jnp.concatenate(
            [media_pair[depth].reshape(samples, media_len, -1), latent_pair.reshape(samples, latent_rows, -1)], axis=1
        )
        keys, values = heads_of(pair[..., :wide]), heads_of(pair[..., wide:])
        scores = score_block(queries, keys)
        row_max = jnp.max(scores, axis=-1, keepdims=True)
        exp_scores = jnp.exp(scores - row_max)
        row_total = jnp.sum(exp_scores, axis=-1, keepdims=True)
        probs = exp_scores / row_total
        log_total = row_max + jnp.log(row_total)
        attended = jnp.einsum("shqk,skhd->sqhd", probs.astype(BF16), values, preferred_element_type=F32)
        attended = attended.astype(BF16).reshape(rows, wide)
        middle = state + links.core_sum(mm_bt(attended, out4[depth]))
        ff_normed, ff_rstd = normalize(middle)
        ff_x = (ff_normed * ff_gain[depth] + ff_bias[depth]).astype(BF16)
        up_pre = mm(ff_x, w_up[depth])
        hidden = jax.nn.gelu(up_pre, approximate=False).astype(BF16)
        state = middle + links.tensor_sum(mm(hidden, w_down[depth]))
        saved.append(
            (latent_normed, latent_rstd, latent_x, queries, keys, values, log_total, attended,
             ff_normed, ff_rstd, ff_x, up_pre, hidden)
        )

    upstream = cotangent.reshape(rows, width)
    grads = [None] * layers
    gains = [None] * layers
    pair_grads = [None] * layers
    for depth in reversed(range(layers)):
        (latent_normed, latent_rstd, latent_x, queries, keys, values, log_total, attended,
         ff_normed, ff_rstd, ff_x, up_pre, hidden) = saved[depth]
        upstream_low = upstream.astype(BF16)
        down_left = links.side_rows(hidden)
        down_right = links.side_columns(upstream_low)
        grad_down = links.line_scatter(lambda i: mm_at(down_left, lax.dynamic_index_in_dim(down_right, i, 0, keepdims=False)))
        grad_pre = (mm_bt(upstream_low, w_down[depth]) * gelu_slope(up_pre)).astype(BF16)
        up_left = links.side_columns(ff_x)
        up_right = links.side_rows(grad_pre)
        grad_up = links.line_scatter(lambda i: mm_at(lax.dynamic_index_in_dim(up_left, i, 0, keepdims=False), up_right))
        grad_ffx = links.tensor_sum(mm_bt(grad_pre, w_up[depth]))
        grad_middle = upstream + norm_back(grad_ffx, ff_gain[depth], ff_normed, ff_rstd)
        middle_low = grad_middle.astype(BF16)
        grad_att = mm(middle_low, out4[depth]).astype(BF16)
        grad_heads = heads_of(grad_att)
        probs = jnp.exp(score_block(queries, keys) - log_total)
        grad_probs = jnp.einsum("sqhd,skhd->shqk", grad_heads, values, preferred_element_type=F32)
        row_delta = jnp.sum(probs * grad_probs, axis=-1, keepdims=True)
        grad_scores = (probs * (grad_probs - row_delta)).astype(BF16)
        grad_query = (
            jnp.einsum("shqk,skhd->sqhd", grad_scores, keys, preferred_element_type=F32) * score_scale
        ).astype(BF16).reshape(rows, wide)
        grad_key = (
            jnp.einsum("shqk,sqhd->skhd", grad_scores, heads_of(queries), preferred_element_type=F32) * score_scale
        ).astype(BF16).reshape(samples, key_count, wide)
        grad_value = jnp.einsum(
            "shqk,sqhd->skhd", probs.astype(BF16), grad_heads, preferred_element_type=F32
        ).astype(BF16).reshape(samples, key_count, wide)
        grad_pair = jnp.concatenate([grad_key, grad_value], axis=-1)
        media_pair_grad = grad_pair[:, :media_len].reshape(samples * media_len, 2 * wide)
        latent_pair_grad = grad_pair[:, media_len:].reshape(rows, 2 * wide)
        pair_grads[depth] = media_pair_grad
        grad_latx = links.core_sum(mm_bt(grad_query, query4[depth]) + mm_bt(latent_pair_grad, pair4[depth]))

        def own_pair(value):
            return jnp.concatenate([value[:, :own], value[:, wide:wide + own]], axis=1)

        media_own = own_pair(media_pair_grad)
        media_w = mm_at(media_x[depth], media_own)
        latent_w = mm_at(latent_x, jnp.concatenate([own_pair(latent_pair_grad), grad_query[:, :own]], axis=1))
        out_w = mm_at(middle_low, attended[:, :own])
        sums = jnp.sum(media_own.astype(F32), axis=0)
        weight_own = jnp.concatenate([w_key[depth], w_value[depth]], axis=1).astype(F32)
        media_gain_part = jnp.sum(weight_own * (media_w - media_bias[depth][:, None] * sums), axis=1) / media_gain[depth]
        media_bias_part = jnp.sum(weight_own * sums, axis=1)
        attn_w = jnp.concatenate([media_w + latent_w[:, :2 * own], latent_w[:, 2 * own:], out_w], axis=1)
        split = attn_w.reshape(links.planes, 2, width // links.dp_size, 4 * own)
        halves = lax.dynamic_index_in_dim(split, links.side, 1, keepdims=False) + links.side_swap(
            lax.dynamic_index_in_dim(split, 1 - links.side, 1, keepdims=False)
        )
        grad_attn = links.line_scatter(lambda i: lax.dynamic_index_in_dim(halves, i, 0, keepdims=False))
        grads[depth] = (grad_attn, grad_up, grad_down)
        upstream = grad_middle + norm_back(grad_latx, latent_gain[depth], latent_normed, latent_rstd)
        share = 1.0 / links.tensor_size
        gains[depth] = (
            media_gain_part,
            media_bias_part,
            jnp.sum(grad_latx * latent_normed, axis=0) * share,
            jnp.sum(grad_latx, axis=0) * share,
            jnp.sum(grad_ffx * ff_normed, axis=0) * share,
            jnp.sum(grad_ffx, axis=0) * share,
        )

    chip_width = width // links.groups
    core_width = width // links.tensor_size

    def chip_columns(value):
        return lax.dynamic_slice_in_dim(value, links.group * chip_width, chip_width, value.ndim - 1)

    total = 0.0
    mean_one = 0.0
    mean_two = 0.0
    for depth in range(layers):
        grad_pair = pair_grads[depth]
        weight = pair4[depth]
        weight_chip = lax.dynamic_slice_in_dim(weight, links.group * chip_width, chip_width, 0)
        total = total + mm_bt(grad_pair, weight_chip) * chip_columns(media_gain[depth])
        weight_long = weight.astype(F32)
        gain_mean = jnp.sum(weight_long * media_gain[depth][:, None], axis=0) / width
        bias_mean = jnp.sum(weight_long * media_bias[depth][:, None], axis=0)
        grad_long = grad_pair.astype(F32)
        mean_one = mean_one + jnp.sum(grad_long * gain_mean, axis=1, keepdims=True)
        mean_two = mean_two + jnp.sum(
            grad_long * (media_pair[depth].astype(F32) - bias_mean), axis=1, keepdims=True
        ) / width
    media_part = media_rstd * (total - mean_one - chip_columns(media_normed) * mean_two)
    mine = lax.dynamic_slice_in_dim(media_part, links.core * core_width, core_width, 1)
    theirs = lax.dynamic_slice_in_dim(media_part, (1 - links.core) * core_width, core_width, 1)
    media_total = mine + links.core_swap(theirs)
    media_grad = media_total.astype(BF16).reshape(samples, media_len, core_width)
    time_part = jnp.sum(media_total.reshape(samples, frames, patches, core_width), axis=(0, 2))

    latent_part = jnp.sum(upstream.reshape(samples, latent_rows, width), axis=0)
    tensor_at = lax.axis_index("tensor")
    latent_share = lax.dynamic_slice_in_dim(latent_part, tensor_at * core_width, core_width, 1)
    gain_flat = jnp.stack([jnp.stack([gains[l][m] for l in range(layers)]) for m in range(6)]).reshape(6 * layers, width)
    gain_split = gain_flat.reshape(6 * layers, links.groups, 2, core_width)
    core_mine = lax.dynamic_index_in_dim(gain_split, links.core, 2, keepdims=False)
    core_theirs = lax.dynamic_index_in_dim(gain_split, 1 - links.core, 2, keepdims=False)
    gain_share = core_mine + links.core_swap(core_theirs)
    gain_sum = lax.dynamic_index_in_dim(gain_share, links.group, 1, keepdims=False)
    for turn in range(1, links.groups):
        target = lax.rem(links.group + turn, links.groups)
        gain_sum = gain_sum + links.group_turn(lax.dynamic_index_in_dim(gain_share, target, 1, keepdims=False), turn)
    small = links.dp_sum(jnp.concatenate([gain_sum, time_part, latent_share], axis=0))
    by_core = jnp.stack([small, links.core_swap(small)])
    by_core = jnp.where(links.core == 0, by_core, by_core[::-1])
    turned = jnp.stack([by_core] + [links.group_turn(by_core, k) for k in range(1, links.groups)])
    order = lax.rem(links.group - jnp.arange(links.groups) + links.groups, links.groups)
    ordered = jnp.take(turned, order, axis=0)
    small_all = jnp.transpose(ordered, (2, 0, 1, 3)).reshape(small.shape[0], width)
    gain_all = small_all[: 6 * layers].reshape(6, layers, width)
    time_grad = small_all[6 * layers : 6 * layers + frames]
    latents_grad = small_all[6 * layers + frames :]

    attn = jnp.stack([grads[l][0] for l in range(layers)])
    return (
        state.reshape(samples, latent_rows, width),
        media_grad,
        time_grad,
        latents_grad,
        gain_all[0],
        gain_all[1],
        gain_all[2],
        gain_all[3],
        gain_all[4],
        gain_all[5],
        attn[..., 2 * own : 3 * own],
        attn[..., :own],
        attn[..., own : 2 * own],
        jnp.transpose(attn[..., 3 * own :], (0, 2, 1)),
        jnp.stack([grads[l][1] for l in range(layers)]),
        jnp.stack([grads[l][2] for l in range(layers)]),
    )


def solution(mesh):
    in_specs = (
        P("dp", None, None),
        P("dp"),
        P(),
        P(),
        P(),
        P(),
        P(),
        P(),
        P(),
        P(),
        P(None, None, "tensor"),
        P(None, None, "tensor"),
        P(None, None, "tensor"),
        P(None, "tensor", None),
        P(None, None, "tensor"),
        P(None, "tensor", None),
        P("dp", None, None),
    )
    out_specs = (
        P("dp", None, None),
        P("dp", None, "tensor"),
        P(),
        P(),
        P(),
        P(),
        P(),
        P(),
        P(),
        P(),
        P(None, "dp", "tensor"),
        P(None, "dp", "tensor"),
        P(None, "dp", "tensor"),
        P(None, "tensor", "dp"),
        P(None, "dp", "tensor"),
        P(None, "tensor", "dp"),
    )
    return jax.shard_map(local, mesh=mesh, in_specs=in_specs, out_specs=out_specs, check_vma=False)
```

time: 1530 us -> 689 us (0.45)
  waiting for transfers between devices: 1160 us -> 95.4 us
  starting transfers between devices: 1.46 us -> 140 us
  local copies, waits for them, and re-layouts: 66.7 us -> 130 us
  matrix products: 120 us -> 175 us
    reduce_scatter x7 -> x0, waiting for transfers between devices: 703 us -> none  [the longest x1 153 us: local(): lax.psum_scatter(stacked[5], 'dp', scatter_dimension=2, tiled=True)]
    psum x9 -> x0, waiting for transfers between devices: 459 us -> none  [the longest x2 260 us: local(): lax.psum((gain_stacks[0], gain_stacks[1], gain_stacks[2] * tensor_share,...]
    ppermute x0 -> x82, starting transfers between devices: none -> 140 us  [the longest x36 103 us: line_scatter(): arrived = lax.ppermute(share, 'dp', pairs)]
    ppermute x0 -> x82, waiting for transfers between devices: none -> 95.4 us  [the longest x14 41.2 us: side_swap(): return lax.ppermute(value, 'dp', [(i, i ^ 1) for i in range(self.dp_size)])]
    dot_general x42 -> x70, matrix products: 120 us -> 175 us  [the longest x34 66.9 us: mm_at(): lax.dot_general(left_side, right_side, (((0,), (0,)), ((), ())), preferre...]
    reduce_sum x7 -> x15, other arithmetic: 74.2 us -> 33.4 us  [the longest x2 14.3 us: local(): jnp.sum(grad_long * (media_pair[depth].astype(F32) - bias_mean), axis=1,...]
    reshape x8 -> x21, local copies, waits for them, and re-layouts: 15.5 us -> 39 us  [the longest x2 10.8 us: local(): grad_value = jnp.einsum('shqk,sqhd->skhd', probs.astype(BF16), grad_heads...]
    dynamic_slice x0 -> x25, local copies, waits for them, and re-layouts: none -> 19 us  [the longest x1 6.01 us: local(): lax.dynamic_slice_in_dim(media_part, (1 - links.core) * core_width, core_...]
  transfers between devices with their start and end apart: 16 -> 82, of which waited for: 15 -> 17; matrix products, arithmetic and copies ran while one was open for 7% -> 60% of each run, Pallas kernels for 0% -> 0%
where the time goes in v1:
time: 689 us; the launch traced here: 682 us
  matrix products  175 us (25%)
  starting transfers between devices  140 us (20%)
  other arithmetic  136 us (20%)
  local copies, waits for them, and re-layouts  130 us (19%)
  waiting for transfers between devices  95.4 us (14%)
    ppermute x36, starting transfers between devices, line_scatter(): arrived = lax.ppermute(share, 'dp', pairs)  103 us
    dot_general x34, matrix products, mm_at(): lax.dot_general(left_side, right_side, (((0,), (0,)), ((), ())), preferre...  66.9 us
    dot_general x12, matrix products, mm(): return jnp.dot(left_side, right_side, preferred_element_type=F32)  43.7 us
    ppermute x14, waiting for transfers between devices, side_swap(): return lax.ppermute(value, 'dp', [(i, i ^ 1) for i in range(self.dp_size)])  41.2 us
    ppermute x36, waiting for transfers between devices, line_scatter(): arrived = lax.ppermute(share, 'dp', pairs)  35.4 us
    dot_general x12, matrix products, mm_bt(): lax.dot_general(left_side, right_side, (((1,), (1,)), ((), ())), preferre...  33 us
    unnamed x417, local copies, waits for them, and re-layouts  30.9 us
    slice x4, local copies, waits for them, and re-layouts, local(): keys, values = (heads_of(pair[..., :wide]), heads_of(pair[..., wide:]))  20 us
  transfers between devices with their start and end apart: 82, of which 17 were waited for; matrix products, arithmetic and copies ran while one was open for 60% of the time, Pallas kernels for 0%

profile of v1, /device:TPU:0, one launch (start us, length us, event | category | flops | bytes accessed | tf_op | source)
XLA Modules:
  0.0 682.5 jit_solution(15174658956768282513)
XLA Ops:
  20.2 8.0 %add_reduce_fusion = f32[3,2048]{1,0:T(4,128)S(1)} fusion(bf16[3,2048,1024]{2,1,0:T(8,128)(2,1)} %param.17, f32[2048,1024]{1,0:T(8,128)S(1)} %bitcast.400), kind=kLoop, calls=%fused_computation.7 | loop fusion | flops 18868224 | bytes 20996096 | tf_op jit(solution)/shard_map/reduce_sum | solution.py:13
  28.3 5.0 multiply_reduce_fusion
  38.9 14.6 %fusion.1 = f32[6144,1024]{1,0:T(8,128)} fusion(bf16[3,2048,1024]{2,1,0:T(8,128)(2,1)} %param.17, f32[6144]{0:T(1024)S(1)} %rsqrt.47, f32[6144]{0:T(1024)S(1)} %div.116, f32[8,1024]{1,0:T(8,128)S(1)} %convert_element_type.281), kind=kLoop, calls=%fused_computation.3 | loop fusion | flops 25165824 | bytes 37830656 | tf_op jit(solution)/shard_map/mul | solution.py:16
  55.8 5.8 collective-permute-done.3
  64.9 15.9 %convolution_convert_fusion.1 = bf16[6144,512]{1,0:T(8,128)(2,1)S(1)} fusion(bf16[1024,512]{0,1:T(8,128)(2,1)S(1)} %get-tuple-element.108, f32[6144,1024]{1,0:T(8,128)} %fusion.1, f32[1024]{0:T(1024)S(1)} %bitcast.503, f32[1024]{0:T(1024)S(1)} %bitcast.495), kind=kOutput, calls=%fused_computation.14 | convolution fusion | flops 6464471040 | bytes 32514048 | tf_op jit(solution)/shard_map/dot_general | solution.py:29
  81.3 4.3 pad_maximum_fusion.2
  85.6 4.2 copy.106
  96.0 5.7 copy.104
  120.6 6.9 %collective-permute-done.11 = f32[512,256]{0,1:T(8,128)S(1)} collective-permute-done((f32[512,256]{0,1:T(8,128)}, f32[512,256]{0,1:T(8,128)S(1)}, u32[]{:S(2)}, u32[]{:S(2)}) %collective-permute-start.11) | collective-permute-done | bytes 524320 | tf_op jit(solution)/shard_map/ppermute | solution.py:73
  131.7 8.1 %collective-permute-done.6 = f32[96,1024]{1,0:T(8,128)S(1)} collective-permute-done((f32[96,1024]{1,0:T(8,128)S(1)}, f32[96,1024]{1,0:T(8,128)S(1)}, u32[]{:S(2)}, u32[]{:S(2)}) %collective-permute-start.6) | collective-permute-done | bytes 393248 | tf_op jit(solution)/shard_map/ppermute | solution.py:70
  139.9 17.7 %convolution_convert_fusion = bf16[6144,512]{1,0:T(8,128)(2,1)} fusion(bf16[1024,512]{0,1:T(8,128)(2,1)S(1)} %get-tuple-element.107, f32[6144,1024]{1,0:T(8,128)} %fusion.1, f32[1024]{0:T(1024)S(1)} %bitcast.508, f32[1024]{0:T(1024)S(1)} %bitcast.498), kind=kOutput, calls=%fused_computation.13 | convolution fusion | flops 6464471040 | bytes 32514048 | tf_op jit(solution)/shard_map/dot_general | solution.py:29
  162.2 5.6 pad_maximum_fusion.1
  167.8 4.2 copy.113
  172.0 5.8 copy.111
  202.1 15.2 %collective-permute-done.73 = f32[192,1024]{1,0:T(8,128)S(1)} collective-permute-done((f32[192,1024]{1,0:T(8,128)S(1)}, f32[192,1024]{1,0:T(8,128)S(1)}, u32[]{:S(2)}, u32[]{:S(2)}) %collective-permute-start.73) | collective-permute-done | bytes 786464 | tf_op jit(solution)/shard_map/ppermute | solution.py:73
  218.8 4.5 collective-permute-start.76
  226.0 7.4 %collective-permute-done.57 = f32[192,1024]{1,0:T(8,128)S(1)} collective-permute-done((f32[192,1024]{1,0:T(8,128)S(1)}, f32[192,1024]{1,0:T(8,128)S(1)}, u32[]{:S(2)}, u32[]{:S(2)}) %collective-permute-start.57) | collective-permute-done | bytes 786464 | tf_op jit(solution)/shard_map/ppermute | solution.py:73
  239.6 5.7 multiply_reduce_fusion.6
  256.5 4.4 copy.120
  261.0 5.4 copy.121
  275.6 4.1 multiply_reduce_fusion.3
  283.3 13.7 %multiply_reduce_fusion.7 = (f32[1024]{0:T(1024)}, f32[1024]{0:T(1024)}, f32[1024,256]{0,1:T(8,128)}) fusion(f32[256]{0:T(256)S(1)} %convert_reduce_fusion, bf16[1024,128]{0,1:T(8,128)(2,1)S(1)} %bitcast.466, bf16[1024,128]{0,1:T(8,128)(2,1)S(1)} %bitcast.463, f32[1024]{0:T(1024)S(1)} %bitcast.509, f32[1024,384]{0,1:T(8,128)S(1)} %fusion.141, ...), kind=kOutput, calls=%fused_computation.162 | convolution fusion | flops 3249272832 | bytes 30954496 | tf_op jit(solution)/shard_map/dot_general | solution.py:37
  308.7 7.4 %multiply_reduce_fusion.1 = f32[6144]{0:T(1024)} fusion(bf16[6144,512]{1,0:T(8,128)(2,1)} %convolution_convert_fusion, f32[512]{0:T(512)S(1)} %copy-done.178, bf16[3,2048,512]{2,1,0:T(8,128)(2,1)} %copy-done.3), kind=kLoop, calls=%fused_computation.9 | loop fusion | flops 15722496 | bytes 12609536 | tf_op jit(solution)/shard_map/reduce_sum | solution.py:334
  331.0 5.0 collective-permute-start.58
  341.5 7.0 %collective-permute-start.78 = (f32[1024,128]{1,0:T(8,128)}, f32[1024,128]{1,0:T(8,128)}, u32[]{:S(2)}, u32[]{:S(2)}) collective-permute-start(f32[1024,128]{1,0:T(8,128)} %convolution_add_fusion.5), channel_id=1, source_target_pairs={{0,8},{4,12},{8,16},{12,20},{16,24},{20,28},{1,9},{5,13},{9,17},{1... | collective-permute-start | bytes 1572872 | tf_op jit(solution)/shard_map/ppermute | solution.py:128
  371.7 4.4 collective-permute-start.59
  383.5 10.1 %collective-permute-done.40 = f32[128,512]{1,0:T(8,128)S(1)} collective-permute-done((f32[128,512]{1,0:T(8,128)S(1)}, f32[128,512]{1,0:T(8,128)S(1)}, u32[]{:S(2)}, u32[]{:S(2)}) %collective-permute-start.40) | collective-permute-done | bytes 262176 | tf_op jit(solution)/shard_map/ppermute | solution.py:128
  393.6 4.4 collective-permute-start.67
  403.9 10.7 %collective-permute-done.41 = f32[128,512]{1,0:T(8,128)S(1)} collective-permute-done((f32[128,512]{1,0:T(8,128)S(1)}, f32[128,512]{1,0:T(8,128)S(1)}, u32[]{:S(2)}, u32[]{:S(2)}) %collective-permute-start.41) | collective-permute-done | bytes 262176 | tf_op jit(solution)/shard_map/ppermute | solution.py:128
  414.6 5.2 collective-permute-start.60
  424.9 6.0 collective-permute-start.42
  432.2 10.7 %collective-permute-start.68 = (f32[1024,128]{1,0:T(8,128)}, f32[1024,128]{1,0:T(8,128)}, u32[]{:S(2)}, u32[]{:S(2)}) collective-permute-start(f32[1024,128]{1,0:T(8,128)} %convolution_add_fusion.9), channel_id=1, source_target_pairs={{0,8},{4,12},{8,16},{12,20},{1,9},{5,13},{9,17},{13,21},{2,10},{6,... | collective-permute-start | bytes 1572872 | tf_op jit(solution)/shard_map/ppermute | solution.py:128
  449.4 5.7 multiply_reduce_fusion.5
  466.2 4.4 copy.125
  470.6 5.4 copy.126
  481.5 6.8 %fusion.106 = f32[6144,512]{1,0:T(8,128)} fusion(bf16[6144,512]{1,0:T(8,128)(2,1)S(1)} %bitcast.395, bf16[1024,512]{0,1:T(8,128)(2,1)S(1)} %copy-done.33, s32[]{:T(128)S(6)} %select_n.323), kind=kOutput, calls=%fused_computation.325 | convolution fusion | flops 3221225472 | bytes 19398660 | tf_op jit(solution)/shard_map/dot_general | solution.py:33
  493.2 13.3 %multiply_reduce_fusion.8 = (f32[1024]{0:T(1024)S(1)}, f32[1024]{0:T(1024)S(1)}, f32[1024,256]{0,1:T(8,128)}) fusion(f32[256]{0:T(256)S(1)} %convert_reduce_fusion.1, bf16[1024,128]{0,1:T(8,128)(2,1)} %bitcast.460, bf16[1024,128]{0,1:T(8,128)(2,1)} %bitcast.457, f32[1024]{0:T(1024)S(1)} %bitcast.504, f32[1024,384]{0,1:T(8,128)S(1)} %fusion.135, ...), kind=kOutput, calls=%fused_computation.163 | convolution fusion | flops 3249272832 | bytes 30954496 | tf_op jit(solution)/shard_map/dot_general | solution.py:37
  515.8 6.9 %multiply_reduce_fusion.2 = f32[6144]{0:T(1024)S(1)} fusion(bf16[6144,512]{1,0:T(8,128)(2,1)} %copy-done.12, f32[512]{0:T(512)S(1)} %copy-done.177, bf16[3,2048,512]{2,1,0:T(8,128)(2,1)} %copy-done.2), kind=kLoop, calls=%fused_computation.10 | loop fusion | flops 15722496 | bytes 12609536 | tf_op jit(solution)/shard_map/reduce_sum | solution.py:334
  522.7 14.8 %subtract_multiply_fusion = f32[6144,512]{1,0:T(8,128)} fusion(f32[6144,1024]{1,0:T(8,128)} %fusion.1, s32[]{:T(128)S(6)} %select_n.323, f32[6144,512]{1,0:T(8,128)} %fusion.106, bf16[6144,512]{1,0:T(8,128)(2,1)S(1)} %bitcast.399, f32[6144]{0:T(1024)S(1)} %add_multiply_fusion, f32[6144]{0:T(1024)S(1)} %add.736, f32[512]{0:T(512)S(1)} %bitcast.500, ...), kind=kOutput, calls=%fused_computation.8 | convolution fusion | flops 3243245568 | bytes 44643328 | tf_op jit(solution)/shard_map/dot_general | solution.py:33
  537.5 6.0 constant_dynamic-slice_fusion.17
  567.1 5.5 collective-permute-start.69
  578.5 5.3 collective-permute-start.49
  604.2 4.4 collective-permute-start.34
  609.7 10.4 %collective-permute-done.34 = f32[128,512]{1,0:T(8,128)S(1)} collective-permute-done((f32[128,512]{1,0:T(8,128)S(1)}, f32[128,512]{1,0:T(8,128)S(1)}, u32[]{:S(2)}, u32[]{:S(2)}) %collective-permute-start.34) | collective-permute-done | bytes 262176 | tf_op jit(solution)/shard_map/ppermute | solution.py:128
  622.1 5.8 collective-permute-start.51
  630.3 5.3 collective-permute-start.35
  637.8 9.3 %fusion.336 = (bf16[6144,256]{1,0:T(8,128)(2,1)}, f32[6144,256]{1,0:T(8,128)}) fusion(f32[6144,256]{1,0:T(8,128)} %collective-permute-done.23, f32[6144,512]{1,0:T(8,128)} %subtract_multiply_fusion, s32[]{:T(128)S(6)} %select_n.324), kind=kLoop, calls=%fused_computation.678 | loop fusion | flops 3145728 | bytes 22020100 | tf_op jit(solution)/shard_map/convert_element_type | solution.py:341
  670.4 5.1 collective-permute-done.31
  (869 shorter events, 320.2 us)
Async XLA Ops:
  4.2 31.7 %collective-permute-start = (f32[512,256]{0,1:T(8,128)}, f32[512,256]{0,1:T(8,128)}, u32[]{:S(2)}, u32[]{:S(2)}) collective-permute-start(f32[512,256]{0,1:T(8,128)} %constant_dynamic-slice_fusion.25), channel_id=1, source_target_pairs={{0,2},{1,3},{2,0},{3,1},{4,6},{5,7},{6,4},{7,5},{8,10},{9,11},{10,... | collective-permute-start | bytes 1572872 | tf_op jit(solution)/shard_map/ppermute | solution.py:70
  10.1 25.9 %collective-permute-start.2 = (f32[512,256]{0,1:T(8,128)}, f32[512,256]{0,1:T(8,128)}, u32[]{:S(2)}, u32[]{:S(2)}) collective-permute-start(f32[512,256]{0,1:T(8,128)} %fusion.119), channel_id=1, source_target_pairs={{0,2},{1,3},{2,0},{3,1},{4,6},{5,7},{6,4},{7,5},{8,10},{9,11},{10,... | collective-permute-start | bytes 1572872 | tf_op jit(solution)/shard_map/ppermute | solution.py:70
  11.5 43.0 %collective-permute-start.8 = (f32[512,256]{0,1:T(8,128)}, f32[512,256]{0,1:T(8,128)}, u32[]{:S(2)}, u32[]{:S(2)}) collective-permute-start(f32[512,256]{0,1:T(8,128)} %constant_dynamic-slice_fusion.23), channel_id=1, source_target_pairs={{0,2},{1,3},{2,0},{3,1},{4,6},{5,7},{6,4},{7,5},{8,10},{9,11},{10,... | collective-permute-start | bytes 1572872 | tf_op jit(solution)/shard_map/ppermute | solution.py:70
  14.5 98.3 %collective-permute-start.10 = (f32[512,256]{0,1:T(8,128)}, f32[512,256]{0,1:T(8,128)}, u32[]{:S(2)}, u32[]{:S(2)}) collective-permute-start(f32[512,256]{0,1:T(8,128)} %fusion.117), channel_id=1, source_target_pairs={{0,2},{1,3},{2,0},{3,1},{4,6},{5,7},{6,4},{7,5},{8,10},{9,11},{10,... | collective-permute-start | bytes 1572872 | tf_op jit(solution)/shard_map/ppermute | solution.py:70
  15.6 38.8 %collective-permute-start.74 = (f32[96,4,128]{2,0,1:T(8,128)S(1)}, f32[96,4,128]{2,0,1:T(8,128)}, u32[]{:S(2)}, u32[]{:S(2)}) collective-permute-start(f32[96,4,128]{2,0,1:T(8,128)S(1)} %bitcast.477), channel_id=1, source_target_pairs={{0,4},{4,0},{8,12},{12,8},{16,20},{20,16},{24,28},{28,24},{1,5},{5... | collective-permute-start | bytes 589832 | tf_op jit(solution)/shard_map/ppermute | solution.py:73
  36.0 18.6 %collective-permute-start.1 = (f32[512,256]{0,1:T(8,128)}, f32[512,256]{0,1:T(8,128)S(1)}, u32[]{:S(2)}, u32[]{:S(2)}) collective-permute-start(f32[512,256]{0,1:T(8,128)} %collective-permute-done), channel_id=1, source_target_pairs={{0,4},{4,0},{8,12},{12,8},{16,20},{20,16},{24,28},{28,24},{1,5},{5... | collective-permute-start | bytes 1572872 | tf_op jit(solution)/shard_map/ppermute | solution.py:73
  36.0 25.5 %collective-permute-start.3 = (f32[512,256]{0,1:T(8,128)}, f32[512,256]{0,1:T(8,128)S(1)}, u32[]{:S(2)}, u32[]{:S(2)}) collective-permute-start(f32[512,256]{0,1:T(8,128)} %collective-permute-done.2), channel_id=1, source_target_pairs={{0,4},{4,0},{8,12},{12,8},{16,20},{20,16},{24,28},{28,24},{1,5},{5... | collective-permute-start | bytes 1572872 | tf_op jit(solution)/shard_map/ppermute | solution.py:73
  54.5 56.7 %collective-permute-start.75 = (f32[96,4,128]{2,0,1:T(8,128)}, f32[96,4,128]{2,0,1:T(8,128)}, u32[]{:S(2)}, u32[]{:S(2)}) collective-permute-start(f32[96,4,128]{2,0,1:T(8,128)} %collective-permute-done.74), channel_id=1, source_target_pairs={{0,1},{1,0},{2,3},{3,2},{4,5},{5,4},{6,7},{7,6},{8,9},{9,8},{10,11... | collective-permute-start | bytes 589832 | tf_op jit(solution)/shard_map/ppermute | solution.py:66
  54.5 58.8 %collective-permute-start.9 = (f32[512,256]{0,1:T(8,128)}, f32[512,256]{0,1:T(8,128)}, u32[]{:S(2)}, u32[]{:S(2)}) collective-permute-start(f32[512,256]{0,1:T(8,128)} %collective-permute-done.8), channel_id=1, source_target_pairs={{0,4},{4,0},{8,12},{12,8},{16,20},{20,16},{24,28},{28,24},{1,5},{5... | collective-permute-start | bytes 1572872 | tf_op jit(solution)/shard_map/ppermute | solution.py:73
  139.8 18.9 %collective-permute-start.7 = (f32[96,1024]{1,0:T(8,128)S(1)}, f32[96,1024]{1,0:T(8,128)S(1)}, u32[]{:S(2)}, u32[]{:S(2)}) collective-permute-start(f32[96,1024]{1,0:T(8,128)S(1)} %add.698), channel_id=1, source_target_pairs={{0,1},{1,0},{2,3},{3,2},{4,5},{5,4},{6,7},{7,6},{8,9},{9,8},{10,11... | collective-permute-start | bytes 1179656 | tf_op jit(solution)/shard_map/ppermute | solution.py:66
  158.4 30.7 %collective-permute-start.64 = (f32[192,1024]{1,0:T(8,128)}, f32[192,1024]{1,0:T(8,128)}, u32[]{:S(2)}, u32[]{:S(2)}) collective-permute-start(f32[192,1024]{1,0:T(8,128)} %get-tuple-element.86), channel_id=1, source_target_pairs={{0,4},{4,0},{8,12},{12,8},{16,20},{20,16},{24,28},{28,24},{1,5},{5... | collective-permute-start | bytes 2359304 | tf_op jit(solution)/shard_map/ppermute | solution.py:73
  196.9 20.4 %collective-permute-start.73 = (f32[192,1024]{1,0:T(8,128)S(1)}, f32[192,1024]{1,0:T(8,128)S(1)}, u32[]{:S(2)}, u32[]{:S(2)}) collective-permute-start(f32[192,1024]{1,0:T(8,128)S(1)} %get-tuple-element.90), channel_id=1, source_target_pairs={{0,4},{4,0},{8,12},{12,8},{16,20},{20,16},{24,28},{28,24},{1,5},{5... | collective-permute-start | bytes 2359304 | tf_op jit(solution)/shard_map/ppermute | solution.py:73
  198.8 34.7 %collective-permute-start.57 = (f32[192,1024]{1,0:T(8,128)S(1)}, f32[192,1024]{1,0:T(8,128)S(1)}, u32[]{:S(2)}, u32[]{:S(2)}) collective-permute-start(f32[192,1024]{1,0:T(8,128)S(1)} %get-tuple-element.222), channel_id=1, source_target_pairs={{0,4},{4,0},{8,12},{12,8},{16,20},{20,16},{24,28},{28,24},{1,5},{5... | collective-permute-start | bytes 2359304 | tf_op jit(solution)/shard_map/ppermute | solution.py:73
  199.3 18.2 %collective-permute-start.17 = (f32[96,1024]{1,0:T(8,128)S(1)}, f32[96,1024]{1,0:T(8,128)S(1)}, u32[]{:S(2)}, u32[]{:S(2)}) collective-permute-start(f32[96,1024]{1,0:T(8,128)S(1)} %dynamic-slice_add_fusion.2), channel_id=1, source_target_pairs={{0,2},{1,3},{2,0},{3,1},{4,6},{5,7},{6,4},{7,5},{8,10},{9,11},{10,... | collective-permute-start | bytes 1179656 | tf_op jit(solution)/shard_map/ppermute | solution.py:70
  201.1 33.2 %collective-permute-start.14 = (f32[96,1024]{1,0:T(8,128)S(1)}, f32[96,1024]{1,0:T(8,128)S(1)}, u32[]{:S(2)}, u32[]{:S(2)}) collective-permute-start(f32[96,1024]{1,0:T(8,128)S(1)} %dynamic-slice_add_fusion.3), channel_id=1, source_target_pairs={{0,2},{1,3},{2,0},{3,1},{4,6},{5,7},{6,4},{7,5},{8,10},{9,11},{10,... | collective-permute-start | bytes 1179656 | tf_op jit(solution)/shard_map/ppermute | solution.py:70
  217.5 16.9 %collective-permute-start.18 = (f32[96,1024]{1,0:T(8,128)S(1)}, f32[96,1024]{1,0:T(8,128)S(1)}, u32[]{:S(2)}, u32[]{:S(2)}) collective-permute-start(f32[96,1024]{1,0:T(8,128)S(1)} %add.722), channel_id=1, source_target_pairs={{0,1},{1,0},{2,3},{3,2},{4,5},{5,4},{6,7},{7,6},{8,9},{9,8},{10,11... | collective-permute-start | bytes 1179656 | tf_op jit(solution)/shard_map/ppermute | solution.py:66
  218.8 102.5 %collective-permute-start.76 = (f32[1024,128]{1,0:T(8,128)}, f32[1024,128]{1,0:T(8,128)}, u32[]{:S(2)}, u32[]{:S(2)}) collective-permute-start(f32[1024,128]{1,0:T(8,128)} %fusion.166), channel_id=1, source_target_pairs={{0,8},{4,12},{1,9},{5,13},{2,10},{6,14},{3,11},{7,15}} | collective-permute-start | bytes 1572872 | tf_op jit(solution)/shard_map/ppermute | solution.py:128
  224.6 102.0 %collective-permute-start.79 = (f32[1024,128]{1,0:T(8,128)}, f32[1024,128]{1,0:T(8,128)}, u32[]{:S(2)}, u32[]{:S(2)}) collective-permute-start(f32[1024,128]{1,0:T(8,128)} %fusion.153), channel_id=1, source_target_pairs={{24,16},{28,20},{25,17},{29,21},{26,18},{30,22},{27,19},{31,23}} | collective-permute-start | bytes 1572872 | tf_op jit(solution)/shard_map/ppermute | solution.py:128
  269.2 80.6 %collective-permute-start.19 = (f32[192,1024]{1,0:T(8,128)}, f32[192,1024]{1,0:T(8,128)}, u32[]{:S(2)}, u32[]{:S(2)}) collective-permute-start(f32[192,1024]{1,0:T(8,128)} %convolution_add_fusion.1), channel_id=1, source_target_pairs={{0,1},{1,0},{2,3},{3,2},{4,5},{5,4},{6,7},{7,6},{8,9},{9,8},{10,11... | collective-permute-start | bytes 2359304 | tf_op jit(solution)/shard_map/ppermute | solution.py:66
  274.0 52.6 %collective-permute-start.55 = (f32[96,4,128]{2,0,1:T(8,128)}, f32[96,4,128]{2,0,1:T(8,128)}, u32[]{:S(2)}, u32[]{:S(2)}) collective-permute-start(f32[96,4,128]{2,0,1:T(8,128)} %bitcast.384), channel_id=1, source_target_pairs={{0,4},{4,0},{8,12},{12,8},{16,20},{20,16},{24,28},{28,24},{1,5},{5... | collective-permute-start | bytes 589832 | tf_op jit(solution)/shard_map/ppermute | solution.py:73
  308.4 61.8 %collective-permute-start.39 = (f32[4,128,512]{2,1,0:T(8,128)}, f32[4,128,512]{2,1,0:T(8,128)}, u32[]{:S(2)}, u32[]{:S(2)}) collective-permute-start(f32[4,128,512]{2,1,0:T(8,128)} %bitcast.103), channel_id=1, source_target_pairs={{0,4},{4,0},{8,12},{12,8},{16,20},{20,16},{24,28},{28,24},{1,5},{5... | collective-permute-start | bytes 3145736 | tf_op jit(solution)/shard_map/ppermute | solution.py:73
  331.0 31.4 %collective-permute-start.58 = (f32[128,1024]{1,0:T(8,128)}, f32[128,1024]{1,0:T(8,128)}, u32[]{:S(2)}, u32[]{:S(2)}) collective-permute-start(f32[128,1024]{1,0:T(8,128)} %fusion.212), channel_id=1, source_target_pairs={{0,8},{4,12},{1,9},{5,13},{2,10},{6,14},{3,11},{7,15}} | collective-permute-start | bytes 1572872 | tf_op jit(solution)/shard_map/ppermute | solution.py:128
  338.8 26.4 %collective-permute-start.61 = (f32[128,1024]{1,0:T(8,128)}, f32[128,1024]{1,0:T(8,128)}, u32[]{:S(2)}, u32[]{:S(2)}) collective-permute-start(f32[128,1024]{1,0:T(8,128)} %fusion.199), channel_id=1, source_target_pairs={{24,16},{28,20},{25,17},{29,21},{26,18},{30,22},{27,19},{31,23}} | collective-permute-start | bytes 1572872 | tf_op jit(solution)/shard_map/ppermute | solution.py:128
  341.5 30.2 %collective-permute-start.78 = (f32[1024,128]{1,0:T(8,128)}, f32[1024,128]{1,0:T(8,128)}, u32[]{:S(2)}, u32[]{:S(2)}) collective-permute-start(f32[1024,128]{1,0:T(8,128)} %convolution_add_fusion.5), channel_id=1, source_target_pairs={{0,8},{4,12},{8,16},{12,20},{16,24},{20,28},{1,9},{5,13},{9,17},{1... | collective-permute-start | bytes 1572872 | tf_op jit(solution)/shard_map/ppermute | solution.py:128
  349.7 26.4 %collective-permute-start.81 = (f32[1024,128]{1,0:T(8,128)}, f32[1024,128]{1,0:T(8,128)}, u32[]{:S(2)}, u32[]{:S(2)}) collective-permute-start(f32[1024,128]{1,0:T(8,128)} %convolution_add_fusion.3), channel_id=1, source_target_pairs={{24,16},{28,20},{16,8},{20,12},{8,0},{12,4},{25,17},{29,21},{17,9}... | collective-permute-start | bytes 1572872 | tf_op jit(solution)/shard_map/ppermute | solution.py:128
  368.7 53.3 %collective-permute-start.48 = (f32[192,1024]{1,0:T(8,128)S(1)}, f32[192,1024]{1,0:T(8,128)S(1)}, u32[]{:S(2)}, u32[]{:S(2)}) collective-permute-start(f32[192,1024]{1,0:T(8,128)S(1)} %get-tuple-element.224), channel_id=1, source_target_pairs={{0,4},{4,0},{8,12},{12,8},{16,20},{20,16},{24,28},{28,24},{1,5},{5... | collective-permute-start | bytes 2359304 | tf_op jit(solution)/shard_map/ppermute | solution.py:73
  371.7 26.3 %collective-permute-start.59 = (f32[128,1024]{1,0:T(8,128)S(1)}, f32[128,1024]{1,0:T(8,128)S(1)}, u32[]{:S(2)}, u32[]{:S(2)}) collective-permute-start(f32[128,1024]{1,0:T(8,128)S(1)} %convolution_add_fusion.14), channel_id=1, source_target_pairs={{0,8},{4,12},{8,16},{12,20},{1,9},{5,13},{9,17},{13,21},{2,10},{6,... | collective-permute-start | bytes 1572872 | tf_op jit(solution)/shard_map/ppermute | solution.py:128
  376.2 24.3 %collective-permute-start.62 = (f32[128,1024]{1,0:T(8,128)S(1)}, f32[128,1024]{1,0:T(8,128)S(1)}, u32[]{:S(2)}, u32[]{:S(2)}) collective-permute-start(f32[128,1024]{1,0:T(8,128)S(1)} %convolution_add_fusion.12), channel_id=1, source_target_pairs={{24,16},{28,20},{16,8},{20,12},{25,17},{29,21},{17,9},{21,13},{26,... | collective-permute-start | bytes 1572872 | tf_op jit(solution)/shard_map/ppermute | solution.py:128
  381.8 21.4 %collective-permute-start.43 = (f32[128,512]{1,0:T(8,128)S(1)}, f32[128,512]{1,0:T(8,128)S(1)}, u32[]{:S(2)}, u32[]{:S(2)}) collective-permute-start(f32[128,512]{1,0:T(8,128)S(1)} %get-tuple-element.131), channel_id=1, source_target_pairs={{24,16},{28,20},{25,17},{29,21},{26,18},{30,22},{27,19},{31,23}} | collective-permute-start | bytes 786440 | tf_op jit(solution)/shard_map/ppermute | solution.py:128
  393.6 29.3 %collective-permute-start.67 = (f32[1024,128]{1,0:T(8,128)S(1)}, f32[1024,128]{1,0:T(8,128)S(1)}, u32[]{:S(2)}, u32[]{:S(2)}) collective-permute-start(f32[1024,128]{1,0:T(8,128)S(1)} %fusion.189), channel_id=1, source_target_pairs={{0,8},{4,12},{1,9},{5,13},{2,10},{6,14},{3,11},{7,15}} | collective-permute-start | bytes 1572872 | tf_op jit(solution)/shard_map/ppermute | solution.py:128
  400.5 20.1 %collective-permute-start.21 = (f32[96,1024]{1,0:T(8,128)S(1)}, f32[96,1024]{1,0:T(8,128)S(1)}, u32[]{:S(2)}, u32[]{:S(2)}) collective-permute-start(f32[96,1024]{1,0:T(8,128)S(1)} %dynamic-slice_add_fusion.1), channel_id=1, source_target_pairs={{0,2},{1,3},{2,0},{3,1},{4,6},{5,7},{6,4},{7,5},{8,10},{9,11},{10,... | collective-permute-start | bytes 1179656 | tf_op jit(solution)/shard_map/ppermute | solution.py:70
  403.2 21.8 %collective-permute-start.70 = (f32[1024,128]{1,0:T(8,128)S(1)}, f32[1024,128]{1,0:T(8,128)S(1)}, u32[]{:S(2)}, u32[]{:S(2)}) collective-permute-start(f32[1024,128]{1,0:T(8,128)S(1)} %fusion.176), channel_id=1, source_target_pairs={{24,16},{28,20},{25,17},{29,21},{26,18},{30,22},{27,19},{31,23}} | collective-permute-start | bytes 1572872 | tf_op jit(solution)/shard_map/ppermute | solution.py:128
  414.6 130.5 %collective-permute-start.60 = (f32[128,1024]{1,0:T(8,128)}, f32[128,1024]{1,0:T(8,128)}, u32[]{:S(2)}, u32[]{:S(2)}) collective-permute-start(f32[128,1024]{1,0:T(8,128)} %convolution_add_fusion.15), channel_id=1, source_target_pairs={{0,8},{4,12},{8,16},{12,20},{16,24},{20,28},{1,9},{5,13},{9,17},{1... | collective-permute-start | bytes 1572872 | tf_op jit(solution)/shard_map/ppermute | solution.py:128
  420.6 125.8 %collective-permute-start.63 = (f32[128,1024]{1,0:T(8,128)}, f32[128,1024]{1,0:T(8,128)}, u32[]{:S(2)}, u32[]{:S(2)}) collective-permute-start(f32[128,1024]{1,0:T(8,128)} %convolution_add_fusion.13), channel_id=1, source_target_pairs={{24,16},{28,20},{16,8},{20,12},{8,0},{12,4},{25,17},{29,21},{17,9}... | collective-permute-start | bytes 1572872 | tf_op jit(solution)/shard_map/ppermute | solution.py:128
  422.0 21.7 %collective-permute-start.22 = (f32[96,1024]{1,0:T(8,128)S(1)}, f32[96,1024]{1,0:T(8,128)S(1)}, u32[]{:S(2)}, u32[]{:S(2)}) collective-permute-start(f32[96,1024]{1,0:T(8,128)S(1)} %add.731), channel_id=1, source_target_pairs={{0,1},{1,0},{2,3},{3,2},{4,5},{5,4},{6,7},{7,6},{8,9},{9,8},{10,11... | collective-permute-start | bytes 1179656 | tf_op jit(solution)/shard_map/ppermute | solution.py:66
  424.9 131.6 %collective-permute-start.42 = (f32[128,512]{1,0:T(8,128)}, f32[128,512]{1,0:T(8,128)}, u32[]{:S(2)}, u32[]{:S(2)}) collective-permute-start(f32[128,512]{1,0:T(8,128)} %get-tuple-element.128), channel_id=1, source_target_pairs={{0,8},{4,12},{8,16},{12,20},{16,24},{20,28},{1,9},{5,13},{9,17},{1... | collective-permute-start | bytes 786440 | tf_op jit(solution)/shard_map/ppermute | solution.py:128
  432.2 132.0 %collective-permute-start.68 = (f32[1024,128]{1,0:T(8,128)}, f32[1024,128]{1,0:T(8,128)}, u32[]{:S(2)}, u32[]{:S(2)}) collective-permute-start(f32[1024,128]{1,0:T(8,128)} %convolution_add_fusion.9), channel_id=1, source_target_pairs={{0,8},{4,12},{8,16},{12,20},{1,9},{5,13},{9,17},{13,21},{2,10},{6,... | collective-permute-start | bytes 1572872 | tf_op jit(solution)/shard_map/ppermute | solution.py:128
  443.7 123.4 %collective-permute-start.71 = (f32[1024,128]{1,0:T(8,128)}, f32[1024,128]{1,0:T(8,128)}, u32[]{:S(2)}, u32[]{:S(2)}) collective-permute-start(f32[1024,128]{1,0:T(8,128)} %convolution_add_fusion.7), channel_id=1, source_target_pairs={{24,16},{28,20},{16,8},{20,12},{25,17},{29,21},{17,9},{21,13},{26,... | collective-permute-start | bytes 1572872 | tf_op jit(solution)/shard_map/ppermute | solution.py:128
  546.4 91.4 %collective-permute-start.23 = (f32[6144,256]{1,0:T(8,128)}, f32[6144,256]{1,0:T(8,128)}, u32[]{:S(2)}, u32[]{:S(2)}) collective-permute-start(f32[6144,256]{1,0:T(8,128)} %constant_dynamic-slice_fusion.17), channel_id=1, source_target_pairs={{0,1},{1,0},{2,3},{3,2},{4,5},{5,4},{6,7},{7,6},{8,9},{9,8},{10,11... | collective-permute-start | bytes 18874376 | tf_op jit(solution)/shard_map/ppermute | solution.py:66
  557.1 36.6 %collective-permute-start.32 = (f32[4,128,512]{2,1,0:T(8,128)}, f32[4,128,512]{2,1,0:T(8,128)}, u32[]{:S(2)}, u32[]{:S(2)}) collective-permute-start(f32[4,128,512]{2,1,0:T(8,128)} %bitcast.472), channel_id=1, source_target_pairs={{0,4},{4,0},{8,12},{12,8},{16,20},{20,16},{24,28},{28,24},{1,5},{5... | collective-permute-start | bytes 3145736 | tf_op jit(solution)/shard_map/ppermute | solution.py:73
  567.1 23.1 %collective-permute-start.69 = (f32[1024,128]{1,0:T(8,128)}, f32[1024,128]{1,0:T(8,128)}, u32[]{:S(2)}, u32[]{:S(2)}) collective-permute-start(f32[1024,128]{1,0:T(8,128)} %convolution_add_fusion.10), channel_id=1, source_target_pairs={{0,8},{4,12},{8,16},{12,20},{16,24},{20,28},{1,9},{5,13},{9,17},{1... | collective-permute-start | bytes 1572872 | tf_op jit(solution)/shard_map/ppermute | solution.py:128
  578.5 19.9 %collective-permute-start.49 = (f32[128,1024]{1,0:T(8,128)}, f32[128,1024]{1,0:T(8,128)}, u32[]{:S(2)}, u32[]{:S(2)}) collective-permute-start(f32[128,1024]{1,0:T(8,128)} %fusion.235), channel_id=1, source_target_pairs={{0,8},{4,12},{1,9},{5,13},{2,10},{6,14},{3,11},{7,15}} | collective-permute-start | bytes 1572872 | tf_op jit(solution)/shard_map/ppermute | solution.py:128
  599.8 21.1 %collective-permute-start.50 = (f32[128,1024]{1,0:T(8,128)S(1)}, f32[128,1024]{1,0:T(8,128)S(1)}, u32[]{:S(2)}, u32[]{:S(2)}) collective-permute-start(f32[128,1024]{1,0:T(8,128)S(1)} %convolution_add_fusion.19), channel_id=1, source_target_pairs={{0,8},{4,12},{8,16},{12,20},{1,9},{5,13},{9,17},{13,21},{2,10},{6,... | collective-permute-start | bytes 1572872 | tf_op jit(solution)/shard_map/ppermute | solution.py:128
  609.0 18.9 %collective-permute-start.53 = (f32[128,1024]{1,0:T(8,128)S(1)}, f32[128,1024]{1,0:T(8,128)S(1)}, u32[]{:S(2)}, u32[]{:S(2)}) collective-permute-start(f32[128,1024]{1,0:T(8,128)S(1)} %convolution_add_fusion.17), channel_id=1, source_target_pairs={{24,16},{28,20},{16,8},{20,12},{25,17},{29,21},{17,9},{21,13},{26,... | collective-permute-start | bytes 1572872 | tf_op jit(solution)/shard_map/ppermute | solution.py:128
  622.1 28.8 %collective-permute-start.51 = (f32[128,1024]{1,0:T(8,128)}, f32[128,1024]{1,0:T(8,128)}, u32[]{:S(2)}, u32[]{:S(2)}) collective-permute-start(f32[128,1024]{1,0:T(8,128)} %convolution_add_fusion.20), channel_id=1, source_target_pairs={{0,8},{4,12},{8,16},{12,20},{16,24},{20,28},{1,9},{5,13},{9,17},{1... | collective-permute-start | bytes 1572872 | tf_op jit(solution)/shard_map/ppermute | solution.py:128
  629.0 21.9 %collective-permute-start.54 = (f32[128,1024]{1,0:T(8,128)}, f32[128,1024]{1,0:T(8,128)}, u32[]{:S(2)}, u32[]{:S(2)}) collective-permute-start(f32[128,1024]{1,0:T(8,128)} %convolution_add_fusion.18), channel_id=1, source_target_pairs={{24,16},{28,20},{16,8},{20,12},{8,0},{12,4},{25,17},{29,21},{17,9}... | collective-permute-start | bytes 1572872 | tf_op jit(solution)/shard_map/ppermute | solution.py:128
  630.3 33.2 %collective-permute-start.35 = (f32[128,512]{1,0:T(8,128)S(1)}, f32[128,512]{1,0:T(8,128)}, u32[]{:S(2)}, u32[]{:S(2)}) collective-permute-start(f32[128,512]{1,0:T(8,128)S(1)} %get-tuple-element.133), channel_id=1, source_target_pairs={{0,8},{4,12},{8,16},{12,20},{16,24},{20,28},{1,9},{5,13},{9,17},{1... | collective-permute-start | bytes 786440 | tf_op jit(solution)/shard_map/ppermute | solution.py:128
  636.3 27.2 %collective-permute-start.38 = (f32[128,512]{1,0:T(8,128)}, f32[128,512]{1,0:T(8,128)}, u32[]{:S(2)}, u32[]{:S(2)}) collective-permute-start(f32[128,512]{1,0:T(8,128)} %bitcast_add_fusion.10), channel_id=1, source_target_pairs={{24,16},{28,20},{16,8},{20,12},{8,0},{12,4},{25,17},{29,21},{17,9}... | collective-permute-start | bytes 786440 | tf_op jit(solution)/shard_map/ppermute | solution.py:128
  (237 other events, 2570.8 us)

commit v2 on v1

v2 whole, which is shorter than its diff:
```python
import jax
import jax.numpy as jnp
from jax import lax
from jax.experimental import pallas as pl
from jax.experimental.pallas import tpu as pltpu
from jax.sharding import PartitionSpec as P

HEAD_DIM = 64
EPS = 1e-05
F32 = jnp.float32
BF16 = jnp.bfloat16
VMEM_LIMIT = 62 * 1024 * 1024


def mm(left_side, right_side):
    return jnp.dot(left_side, right_side, preferred_element_type=F32)


def mm_bt(left_side, right_side):
    return lax.dot_general(left_side, right_side, (((1,), (1,)), ((), ())), preferred_element_type=F32)


def mm_at(left_side, right_side):
    return lax.dot_general(left_side, right_side, (((0,), (0,)), ((), ())), preferred_element_type=F32)


def dot_rows(left_side, right_side):
    return lax.dot_general(left_side, right_side, (((0,), (0,)), ((), ())), preferred_element_type=F32)


def row_norm(values):
    count = values.shape[-1]
    mean = jnp.sum(values, axis=-1, keepdims=True) * (1.0 / count)
    centered = values - mean
    rstd = lax.rsqrt(jnp.sum(centered * centered, axis=-1, keepdims=True) * (1.0 / count) + EPS)
    return centered * rstd, mean, rstd


def row_norm_back(grad, gain, normed, rstd):
    count = grad.shape[-1]
    scaled = grad * gain
    mean_one = jnp.sum(scaled, axis=-1, keepdims=True) * (1.0 / count)
    mean_two = jnp.sum(scaled * normed, axis=-1, keepdims=True) * (1.0 / count)
    return rstd * (scaled - mean_one - normed * mean_two)


def whole(shape):
    zeros = (0,) * len(shape)
    return pl.BlockSpec(shape, lambda *_: zeros)


def call(body, scalars, grid, ins, outs, scratch, name, flops, moved, exps=0, aliases=None):
    return pl.pallas_call(
        body,
        out_shape=[jax.ShapeDtypeStruct(shape, dtype) for shape, dtype, _ in outs],
        grid_spec=pltpu.PrefetchScalarGridSpec(
            num_scalar_prefetch=len(scalars),
            grid=grid,
            in_specs=[spec for _, spec in ins],
            out_specs=[spec for _, _, spec in outs],
            scratch_shapes=scratch,
        ),
        compiler_params=pltpu.CompilerParams(
            dimension_semantics=("arbitrary",) * len(grid), vmem_limit_bytes=VMEM_LIMIT
        ),
        cost_estimate=pl.CostEstimate(flops=flops, bytes_accessed=moved, transcendentals=exps),
        name=name,
        input_output_aliases=aliases or {},
    )(*scalars, *[array for array, _ in ins])


def frames_in_block(frames):
    return 4 if frames % 4 == 0 else 1


def live_block(group, groups):
    def block(clip, at, counts_ref, *_):
        return (clip * groups + jnp.minimum(at, (counts_ref[clip] - 1) // group), 0)

    return block


def pack(place, wanted, name):
    ins, outs, counts = [], [], []
    for weights, depth, halved in wanted:
        count = weights[0].shape[1] // (2 if halved else 1)
        for weight in weights:
            spec = lambda i, place_ref, depth=depth, halved=halved: (depth, place_ref[2] if halved else 0, 0)
            ins.append((weight, pl.BlockSpec((None, count, weight.shape[2]), spec)))
        shape = (count, sum(weight.shape[2] for weight in weights))
        outs.append((shape, F32, whole(shape)))
        counts.append(len(weights))

    def body(place_ref, *refs):
        in_refs, out_refs = list(refs[: len(ins)]), refs[len(ins) :]
        for out_ref, count in zip(out_refs, counts):
            at = 0
            for _ in range(count):
                part = in_refs.pop(0)
                out_ref[:, at : at + part.shape[1]] = part[...].astype(F32)
                at += part.shape[1]

    moved = sum(6 * shape[0] * shape[1] for shape, _, _ in outs)
    return call(body, [place], (1,), ins, outs, [], name, moved, moved)


def keep_rows(ref, first, columns, side, near, far):
    if far is None:
        ref[first : first + near.shape[0], columns] = near[...].astype(BF16)
        return
    half = near.shape[0]
    ref[pl.ds(pl.multiple_of(first + side * half, half), half), columns] = near[...].astype(BF16)
    ref[pl.ds(pl.multiple_of(first + (1 - side) * half, half), half), columns] = far[...].astype(BF16)


class Gathered:

    def __init__(self, value, groups, turn):
        self.value = value
        self.groups = groups
        self.turn = turn
        self.shape = (value.shape[0] // groups, value.shape[1])

    def spec(self):
        def block(*at):
            return (lax.rem(at[-1][1] + self.groups - self.turn, self.groups), 0)

        return pl.BlockSpec(self.shape, block)


def with_spec(value):
    if isinstance(value, Gathered):
        return (value.value, value.spec())
    return (value, whole(value.shape))


def prepare(media, counts, time_rows, gain, bias, w_key, w_value, depth, turns, frames, patches):
    rows, width = media.shape
    samples = counts.shape[0]
    own = w_key.shape[2]
    group = frames_in_block(frames)
    groups = frames // group

    def body(counts_ref, media_ref, time_ref, gain_ref, bias_ref, wk_ref, wv_ref, x_ref, stat_ref, pair_ref, weight_ref):
        clip, at = pl.program_id(0), pl.program_id(1)

        @pl.when((clip == 0) & (at == 0))
        def _():
            weight_ref[...] = jnp.concatenate([wk_ref[...], wv_ref[...]], axis=1)

        for inner in range(group):
            frame = at * group + inner
            here = slice(inner * patches, (inner + 1) * patches)

            @pl.when(frame < counts_ref[clip])
            def _():
                values = media_ref[here, :].astype(F32) + time_ref[pl.ds(frame, 1), :]
                normed, mean, rstd = row_norm(values)
                x = (normed * gain_ref[...] + bias_ref[...]).astype(BF16)
                x_ref[here, :] = x
                lane = lax.broadcasted_iota(jnp.int32, (patches, 128), 1)
                stat_ref[here, :] = jnp.where(lane < 64, mean, rstd)
                pair_ref[here, :] = jnp.dot(x, weight_ref[...], preferred_element_type=F32).astype(BF16)

            @pl.when((frame >= counts_ref[clip]) & (at * group < counts_ref[clip]))
            def _():
                x_ref[here, :] = jnp.zeros((patches, width), BF16)
                pair_ref[here, :] = jnp.zeros((patches, 2 * own), BF16)

    block = live_block(group, groups)
    deep = group * patches
    row_spec = pl.BlockSpec((deep, width), block)
    weight_spec = pl.BlockSpec((None, width, own), lambda *_: (depth, 0, 0))
    return call(
        body, [counts], (samples, groups),
        [(media, row_spec), (time_rows, whole(time_rows.shape)), (gain, whole(gain.shape)), (bias, whole(bias.shape)),
         (w_key, weight_spec), (w_value, weight_spec)],
        [((rows, width), BF16, row_spec), ((rows, 128), F32, pl.BlockSpec((deep, 128), block)),
         ((rows, 2 * own * turns), BF16, pl.BlockSpec((deep, 2 * own), block)),
         ((width, 2 * own), BF16, whole((width, 2 * own)))],
        [], "prepare", 2 * rows * width * 2 * own, rows * width * 4,
    )


def project_more(media_x, counts, place, pair, near, far, turn, frames, patches):
    rows, width = media_x.shape
    wide = near.shape[1]
    group = frames_in_block(frames)
    groups = frames // group
    parts = 1 if far is None else 2

    def body(counts_ref, place_ref, x_ref, pair_in_ref, *refs):
        out_ref, weight_ref = refs[parts:]
        clip, at = pl.program_id(0), pl.program_id(1)

        @pl.when((clip == 0) & (at == 0))
        def _():
            keep_rows(weight_ref, 0, slice(None), place_ref[2], refs[0], refs[1] if parts == 2 else None)

        for inner in range(group):
            frame = at * group + inner
            here = slice(inner * patches, (inner + 1) * patches)

            @pl.when(frame < counts_ref[clip])
            def _():
                out_ref[here, :] = jnp.dot(x_ref[here, :], weight_ref[...], preferred_element_type=F32).astype(BF16)

            @pl.when((frame >= counts_ref[clip]) & (at * group < counts_ref[clip]))
            def _():
                out_ref[here, :] = jnp.zeros((patches, wide), BF16)

    block = live_block(group, groups)
    deep = group * patches
    halves = [near] if far is None else [near, far]
    return call(
        body, [counts, place], (counts.shape[0], groups),
        [(media_x, pl.BlockSpec((deep, width), block)), (pair, pl.BlockSpec(memory_space=pl.ANY))]
        + [with_spec(half) for half in halves],
        [(pair.shape, BF16, pl.BlockSpec((deep, wide), lambda clip, at, counts_ref, *_: (block(clip, at, counts_ref)[0], turn))),
         ((width, wide), BF16, whole((width, wide)))],
        [], "project_more", 2 * rows * width * wide, 2 * rows * (width + wide), aliases={3: 0},
    )


def spread(rows_of_heads, heads):
    rows, wide = rows_of_heads.shape
    tiled = jnp.concatenate([rows_of_heads] * heads, axis=0)
    head_row = lax.broadcasted_iota(jnp.int32, tiled.shape, 0) // rows
    head_col = lax.broadcasted_iota(jnp.int32, tiled.shape, 1) // (wide // heads)
    return jnp.where(head_row == head_col, tiled, jnp.zeros_like(tiled))


def collect(blocks, heads):
    rows = blocks.shape[0] // heads
    head_col = lax.broadcasted_iota(jnp.int32, (rows, blocks.shape[1]), 1) // (blocks.shape[1] // heads)
    total = jnp.zeros((rows, blocks.shape[1]), blocks.dtype)
    for head in range(heads):
        total = jnp.where(head_col == head, blocks[head * rows : (head + 1) * rows], total)
    return total


def joined(core, mine, other):
    first = core == 0
    return jnp.concatenate([jnp.where(first, mine, other), jnp.where(first, other, mine)], axis=0)


def keys_of(ref, at, own):
    return jnp.concatenate([ref[at, first : first + own] for first in range(0, ref.shape[1], 2 * own)], axis=1)


def values_of(ref, at, own):
    return jnp.concatenate([ref[at, first + own : first + 2 * own] for first in range(0, ref.shape[1], 2 * own)], axis=1)


def attend(state_in, place, counts, gain, bias, w_query, w_out, more, w_pairs, depth, media_pair, latent_rows, frames, patches):
    rows, width = state_in[0].shape
    samples = counts.shape[0]
    own = w_query.shape[2]
    turns = len(w_pairs)
    wide = own * turns
    heads = wide // HEAD_DIM
    scale = HEAD_DIM ** (-0.5)
    media_len = frames * patches
    parts = len(state_in)
    chunk = 2 * patches

    def body(counts_ref, place_ref, *refs):
        state_refs = refs[:parts]
        gain_ref, bias_ref, wq_own_ref, wo_own_ref = refs[parts : parts + 4]
        at_more = parts + 4
        at_pairs = at_more + len(flat)
        more_refs = list(refs[at_more:at_pairs])
        wp_refs = refs[at_pairs : at_pairs + turns]
        pair_ref = refs[at_pairs + turns]
        state_ref, x_ref, q_ref, lat_ref, att_ref, log_ref, part_ref, wq_ref, wo_ref, score_ref = refs[at_pairs + turns + 1 :]
        clip = pl.program_id(0)

        @pl.when(clip == 0)
        def _():
            state = state_refs[0][...]
            if parts == 3:
                state = state + joined(place_ref[0], state_refs[1][...], state_refs[2][...])
            state_ref[...] = state
            normed, _, _ = row_norm(state)
            x = (normed * gain_ref[...] + bias_ref[...]).astype(BF16)
            x_ref[...] = x
            wq_ref[:, :own] = wq_own_ref[...]
            wo_ref[:own, :] = wo_own_ref[...]
            for turn, halves in enumerate(more, 1):
                loaded = [None if half is None else more_refs.pop(0) for half in halves]
                keep_rows(wq_ref, 0, slice(turn * own, (turn + 1) * own), place_ref[2], *loaded[:2])
                keep_rows(wo_ref, turn * own, slice(None), place_ref[2], *loaded[2:])
            q_ref[...] = jnp.dot(x, wq_ref[...], preferred_element_type=F32).astype(BF16)
            for turn in range(turns):
                lat_ref[:, 2 * own * turn : 2 * own * (turn + 1)] = jnp.dot(
                    x, wp_refs[turn][...], preferred_element_type=F32
                ).astype(BF16)

        at = pl.ds(pl.multiple_of(clip * latent_rows, latent_rows), latent_rows)
        queries = spread(q_ref[at, :], heads)
        live = counts_ref[clip] * patches
        chunks = (counts_ref[clip] + 1) // 2

        def rows_of(index):
            return pl.ds(pl.multiple_of(index * chunk, chunk), chunk)

        lat_score = mm_bt(keys_of(lat_ref, at, own), queries) * scale

        def first(index, top):
            score = mm_bt(keys_of(pair_ref, rows_of(index), own), queries) * scale
            row = index * chunk + lax.broadcasted_iota(jnp.int32, score.shape, 0)
            score = jnp.where(row < live, score, -1e30)
            score_ref[rows_of(index), :] = score
            return jnp.maximum(top, jnp.max(score, axis=0, keepdims=True))

        top = lax.fori_loop(0, chunks, first, jnp.max(lat_score, axis=0, keepdims=True))
        lat_exp = jnp.exp(lat_score - top)

        def second(index, total):
            exps = jnp.exp(score_ref[rows_of(index), :] - top)
            score_ref[rows_of(index), :] = exps
            return total + jnp.sum(exps, axis=0, keepdims=True)

        total = lax.fori_loop(0, chunks, second, jnp.sum(lat_exp, axis=0, keepdims=True))
        inverse = 1.0 / total
        log_ref[0] = jnp.broadcast_to(top + jnp.log(total), (8, wide))

        def third(index, sums):
            probs = (score_ref[rows_of(index), :] * inverse).astype(BF16)
            return sums + dot_rows(probs, values_of(pair_ref, rows_of(index), own))

        sums = lax.fori_loop(0, chunks, third, dot_rows((lat_exp * inverse).astype(BF16), values_of(lat_ref, at, own)))
        attended = collect(sums, heads)
        att_ref[...] = attended
        part_ref[...] = jnp.dot(attended.astype(BF16), wo_ref[...], preferred_element_type=F32)

    clip_rows = lambda cols, count: pl.BlockSpec((count, cols), lambda clip, *_: (clip, 0))
    flat = [half for halves in more for half in halves if half is not None]
    ins = [(value, whole(value.shape)) for value in (*state_in, gain, bias)]
    ins += [(w_query, pl.BlockSpec((None, width, own), lambda *_: (depth, 0, 0))),
            (w_out, pl.BlockSpec((None, own, width), lambda *_: (depth, 0, 0)))]
    ins += [with_spec(value) for value in (*flat, *w_pairs)]
    ins.append((media_pair, clip_rows(2 * wide, media_len)))
    outs = [
        ((rows, width), F32, whole((rows, width))),
        ((rows, width), BF16, whole((rows, width))),
        ((rows, wide), BF16, whole((rows, wide))),
        ((rows, 2 * wide), BF16, whole((rows, 2 * wide))),
        ((rows, wide), F32, clip_rows(wide, latent_rows)),
        ((samples, 8, wide), F32, pl.BlockSpec((1, 8, wide), lambda clip, *_: (clip, 0, 0))),
        ((rows, width), F32, clip_rows(width, latent_rows)),
        ((width, wide), BF16, whole((width, wide))),
        ((wide, width), BF16, whole((wide, width))),
    ]
    return call(
        body, [counts, place], (samples,), ins, outs, [pltpu.VMEM((media_len, wide), F32)], "attend",
        2 * samples * media_len * wide * wide * 3, samples * media_len * wide * 4 + 8 * width * wide + 16 * rows * width,
        samples * media_len * wide,
    )


def gelu_parts(values):
    half_more = 0.5 * (1.0 + lax.erf(values * 0.7071067811865476))
    slope = half_more + values * jnp.exp(-0.5 * values * values) * 0.3989422804014327
    return values * half_more, slope


def feed_forward(place, state, part, part_other, gain, bias, w_up, w_down, depth, cotangent=None):
    rows, width = state.shape
    units = w_up.shape[2]
    step = min(256, units)
    steps = units // step
    back = cotangent is not None
    halved = part.shape[0] < rows

    def body(place_ref, state_ref, part_ref, other_ref, gain_ref, bias_ref, up_ref, down_ref, *refs):
        if back:
            cot_ref, mid_ref, x_ref, pre_ref, hid_ref, out_ref, du_ref, dx_ref, dyb_ref = refs
        else:
            mid_ref, x_ref, pre_ref, hid_ref, out_ref = refs
        at = pl.program_id(0)

        @pl.when(at == 0)
        def _():
            if halved:
                middle = state_ref[...] + joined(place_ref[0], part_ref[...], other_ref[...])
            else:
                middle = state_ref[...] + (part_ref[...] + other_ref[...])
            mid_ref[...] = middle
            normed, _, _ = row_norm(middle)
            x_ref[...] = (normed * gain_ref[...] + bias_ref[...]).astype(BF16)
            out_ref[...] = jnp.zeros_like(out_ref)
            if back:
                dx_ref[...] = jnp.zeros_like(dx_ref)
                dyb_ref[...] = cot_ref[...].astype(BF16)

        pre = jnp.dot(x_ref[...], up_ref[...], preferred_element_type=F32)
        pre_ref[...] = pre
        hidden, slope = gelu_parts(pre)
        hidden = hidden.astype(BF16)
        hid_ref[...] = hidden.astype(F32)
        out_ref[...] += jnp.dot(hidden, down_ref[...], preferred_element_type=F32)
        if back:
            du = (mm_bt(dyb_ref[...], down_ref[...]) * slope).astype(BF16)
            du_ref[...] = du.astype(F32)
            dx_ref[...] += mm_bt(du, up_ref[...])

    full = whole((rows, width))
    columns = pl.BlockSpec((rows, step), lambda i, *_: (0, i))
    ins = [(value, whole(value.shape)) for value in (state, part, part_other, gain, bias)]
    ins += [(w_up, pl.BlockSpec((None, width, step), lambda i, *_: (depth, 0, i))), (w_down, pl.BlockSpec((None, step, width), lambda i, *_: (depth, i, 0)))]
    outs = [
        ((rows, width), F32, full),
        ((rows, width), BF16, full),
        ((rows, units), F32, columns),
        ((rows, units), F32, columns),
        ((rows, width), F32, full),
    ]
    scratch = []
    if back:
        ins.append((cotangent, full))
        outs += [((rows, units), F32, columns), ((rows, width), F32, full)]
        scratch = [pltpu.VMEM((rows, width), BF16)]
    return call(
        body, [place], (steps,), ins, outs, scratch, "feed_forward",
        2 * rows * width * units * (4 if back else 2), 4 * width * units + 30 * rows * width, rows * units,
    )


def feed_back(middle_grad, state, grad_x, grad_x_other, gain, pre, w_up, w_down, depth):
    rows, width = state.shape
    units = w_up.shape[2]
    step = min(256, units)
    steps = units // step

    def body(grad_ref, state_ref, gx_ref, gy_ref, gain_ref, pre_ref, up_ref, down_ref, up_out, sums_ref, du_ref, dx_ref, dyb_ref):
        at = pl.program_id(0)

        @pl.when(at == 0)
        def _():
            upstream, sums = latent_back(grad_ref[...], state_ref[...], gx_ref[...] + gy_ref[...], gain_ref[...])
            up_out[...] = upstream
            sums_ref[...] = sums
            dyb_ref[...] = upstream.astype(BF16)
            dx_ref[...] = jnp.zeros_like(dx_ref)

        _, slope = gelu_parts(pre_ref[...])
        du = (mm_bt(dyb_ref[...], down_ref[...]) * slope).astype(BF16)
        du_ref[...] = du.astype(F32)
        dx_ref[...] += mm_bt(du, up_ref[...])

    full = whole((rows, width))
    columns = pl.BlockSpec((rows, step), lambda i: (0, i))
    ins = [(value, whole(value.shape)) for value in (middle_grad, state, grad_x, grad_x_other, gain)]
    ins += [(pre, columns)]
    ins += [(w_up, pl.BlockSpec((None, width, step), lambda i: (depth, 0, i))), (w_down, pl.BlockSpec((None, step, width), lambda i: (depth, i, 0)))]
    return call(
        body, [], (steps,), ins,
        [((rows, width), F32, full), ((8, width), F32, whole((8, width))), ((rows, units), F32, columns), ((rows, width), F32, full)],
        [pltpu.VMEM((rows, width), BF16)], "feed_back",
        4 * rows * width * units, 4 * width * units + 30 * rows * width, rows * units,
    )


def latent_back(middle_grad, state, grad_x, gain):
    normed, _, rstd = row_norm(state)
    upstream = middle_grad + row_norm_back(grad_x, gain, normed, rstd)
    gain_sum = jnp.sum(grad_x * normed, axis=0, keepdims=True)
    bias_sum = jnp.sum(grad_x, axis=0, keepdims=True)
    return upstream, jnp.concatenate([gain_sum, bias_sum, jnp.zeros((6, gain_sum.shape[1]), F32)], axis=0)


def latent_end(middle_grad, state, grad_x, grad_x_other, gain, latent_rows):
    rows, width = state.shape

    def body(grad_ref, state_ref, gx_ref, gy_ref, gain_ref, out_ref):
        upstream, sums = latent_back(grad_ref[...], state_ref[...], gx_ref[...] + gy_ref[...], gain_ref[...])
        total = upstream[:latent_rows]
        for clip in range(1, rows // latent_rows):
            total = total + upstream[clip * latent_rows : (clip + 1) * latent_rows]
        out_ref[...] = jnp.concatenate([sums, total], axis=0)

    ins = [(value, whole(value.shape)) for value in (middle_grad, state, grad_x, grad_x_other, gain)]
    shape = (8 + latent_rows, width)
    return call(body, [], (1,), ins, [(shape, F32, whole(shape))], [], "latent_end", rows * width * 20, rows * width * 16)[0]


def attend_back(
    upstream, middle, grad_mine, grad_other, place, counts, ff_gain, media_gain, media_bias,
    w_query, w_pairs, w_out, w_key, w_value, depth, queries, lat_pair, attended, log_total, latent_x, media_pair, media_x,
    latent_rows, frames, patches,
):
    rows, width = middle.shape
    samples = counts.shape[0]
    wide = w_query.shape[1]
    own = w_key.shape[2]
    turns = len(w_pairs)
    heads = wide // HEAD_DIM
    scale = HEAD_DIM ** (-0.5)
    media_len = frames * patches
    chunk = 2 * patches

    def body(
        counts_ref, place_ref, up_ref, mid_ref, mine_ref, other_ref, ffg_ref, mg_ref, mb_ref,
        wq_ref, wo_ref, *refs,
    ):
        wp_refs = refs[:turns]
        wk_ref, wv_ref, q_ref, lat_ref, att_ref, log_ref, x_ref, pair_ref, mx_ref = refs[turns : turns + 9]
        grad_mid_ref, grad_pair_ref, grad_x_ref, grad_w_ref, sums_ref = refs[turns + 9 : turns + 14]
        low_ref, dq_ref, dlat_ref, col_ref = refs[turns + 14 :]
        clip = pl.program_id(0)

        @pl.when(clip == 0)
        def _():
            grad_x = joined(place_ref[0], mine_ref[...], other_ref[...])
            normed, _, rstd = row_norm(mid_ref[...])
            sums_ref[...] = jnp.zeros_like(sums_ref)
            sums_ref[0:1, :] = jnp.sum(grad_x * normed, axis=0, keepdims=True)
            sums_ref[1:2, :] = jnp.sum(grad_x, axis=0, keepdims=True)
            grad_mid = up_ref[...] + row_norm_back(grad_x, ffg_ref[...], normed, rstd)
            grad_mid_ref[...] = grad_mid
            low_ref[...] = grad_mid.astype(BF16)
            grad_w_ref[...] = jnp.zeros_like(grad_w_ref)
            col_ref[...] = jnp.zeros_like(col_ref)

        at = pl.ds(pl.multiple_of(clip * latent_rows, latent_rows), latent_rows)
        query = spread(q_ref[at, :], heads)
        grad_rows = mm_bt(low_ref[at, :], wo_ref[...]).astype(BF16)
        grad_att = spread(grad_rows, heads)
        cross = spread(grad_rows.astype(F32) * att_ref[at, :], heads)
        cross = jnp.broadcast_to(jnp.sum(cross, axis=1, keepdims=True), (wide, 128))
        delta = jnp.transpose(cross, (1, 0))[0:1, :]
        log = log_ref[0][0:1, :]
        live = counts_ref[clip] * patches
        chunks = (counts_ref[clip] + 1) // 2

        def rows_of(index):
            return pl.ds(pl.multiple_of(index * chunk, chunk), chunk)

        def grads_of(keys, values, row):
            score = mm_bt(keys, query) * scale
            dprob = mm_bt(values, grad_att)
            probs = jnp.exp(score - log)
            if row is not None:
                probs = jnp.where(row < live, probs, 0.0)
            dscore = (probs * (dprob - delta)).astype(BF16)
            grad_key = (jnp.dot(dscore, query, preferred_element_type=F32) * scale).astype(BF16)
            grad_value = jnp.dot(probs.astype(BF16), grad_att, preferred_element_type=F32).astype(BF16)
            grad_pair = []
            for turn in range(turns):
                grad_pair += [grad_key[:, turn * own : (turn + 1) * own], grad_value[:, turn * own : (turn + 1) * own]]
            return dscore, jnp.concatenate(grad_pair, axis=1)

        lat_keys = keys_of(lat_ref, at, own)
        lat_dscore, dlat_ref[at, :] = grads_of(lat_keys, values_of(lat_ref, at, own), None)

        def step(index, dq):
            here = rows_of(index)
            row = index * chunk + lax.broadcasted_iota(jnp.int32, (chunk, wide), 0)
            keys = keys_of(pair_ref, here, own)
            dscore, grad_pair = grads_of(keys, values_of(pair_ref, here, own), row)
            grad_pair_ref[here, :] = grad_pair
            grad_own = grad_pair[:, : 2 * own]
            grad_w_ref[: 2 * own, :] += dot_rows(grad_own, mx_ref[here, :])
            col_ref[0:1, :] += jnp.sum(grad_own.astype(F32), axis=0, keepdims=True)
            return dq + dot_rows(dscore, keys)

        dq = lax.fori_loop(0, chunks, step, dot_rows(lat_dscore, lat_keys))
        dq_ref[at, :] = (collect(dq, heads) * scale).astype(BF16)

        @pl.when(clip == samples - 1)
        def _():
            dq_all = dq_ref[...]
            dlat = dlat_ref[...]
            grad_x = mm_bt(dq_all, wq_ref[...])
            for turn in range(turns):
                grad_x += mm_bt(dlat[:, 2 * own * turn : 2 * own * (turn + 1)], wp_refs[turn][...])
            grad_x_ref[...] = grad_x
            columns = jnp.transpose(col_ref[...], (1, 0))
            total_one = jnp.zeros((1, width), F32)
            total_two = jnp.zeros((1, width), F32)
            for slot, own_ref in enumerate((wk_ref, wv_ref)):
                weight = jnp.transpose(own_ref[...].astype(F32), (1, 0))
                column = columns[slot * own : (slot + 1) * own, 0:1]
                media_w = grad_w_ref[slot * own : (slot + 1) * own, :]
                total_one += jnp.sum(weight * (media_w - column * mb_ref[...]), axis=0, keepdims=True)
                total_two += jnp.sum(weight * column, axis=0, keepdims=True)
            sums_ref[2:3, :] = total_one / mg_ref[...]
            sums_ref[3:4, :] = total_two
            x = x_ref[...]
            grad_w_ref[: 2 * own, :] += dot_rows(dlat[:, : 2 * own], x)
            grad_w_ref[2 * own : 3 * own, :] = dot_rows(dq_all[:, :own], x)
            grad_w_ref[3 * own :, :] = dot_rows(att_ref[:, :own].astype(BF16), low_ref[...])

    clip_rows = lambda cols, count: pl.BlockSpec((count, cols), lambda clip, *_: (clip, 0))
    full = whole((rows, width))
    ins = [(value, whole(value.shape)) for value in (
        upstream, middle, grad_mine, grad_other, ff_gain, media_gain, media_bias,
        w_query, w_out, *w_pairs)]
    ins += [(value, pl.BlockSpec((None, width, own), lambda *_: (depth, 0, 0))) for value in (w_key, w_value)]
    ins += [(value, whole(value.shape)) for value in (queries, lat_pair, attended)]
    ins += [(log_total, pl.BlockSpec((1, 8, wide), lambda clip, *_: (clip, 0, 0))), (latent_x, full)]
    ins += [(media_pair, clip_rows(2 * wide, media_len)), (media_x, clip_rows(width, media_len))]
    outs = [
        ((rows, width), F32, full),
        (media_pair.shape, BF16, clip_rows(2 * wide, media_len)),
        ((rows, width), F32, full),
        ((4 * own, width), F32, whole((4 * own, width))),
        ((8, width), F32, whole((8, width))),
    ]
    scratch = [
        pltpu.VMEM((rows, width), BF16),
        pltpu.VMEM((rows, wide), BF16),
        pltpu.VMEM((rows, 2 * wide), BF16),
        pltpu.VMEM((8, 2 * own), F32),
    ]
    return call(
        body, [counts, place], (samples,), ins, outs, scratch, "attend_back",
        2 * samples * media_len * (5 * wide * wide + 2 * own * width),
        samples * media_len * (8 * wide + 2 * width) + 40 * rows * width, samples * media_len * wide,
    )


def outer_sums(pairs, planes, name):
    count, wide = pairs[0][0].shape
    units = pairs[0][2].shape[1]
    chunk = wide // planes
    step = min(512, units)

    def body(*refs):
        out_ref = refs[-1]
        for pair in range(len(pairs)):
            mine, other, rows, rows_other = [ref[...].astype(BF16) for ref in refs[4 * pair : 4 * pair + 4]]
            total = dot_rows(mine, rows) + dot_rows(other, rows_other)
            for plane in range(planes):
                out_ref[plane, pair] = total[plane * chunk : (plane + 1) * chunk, :]

    ins = []
    for pair in pairs:
        ins += [(value, whole(value.shape)) for value in pair[:2]]
        ins += [(value, pl.BlockSpec((count, step), lambda i: (0, i))) for value in pair[2:]]
    shape = (planes, len(pairs), chunk, units)
    return call(
        body, [], (units // step,), ins,
        [(shape, F32, pl.BlockSpec((planes, len(pairs), chunk, step), lambda i: (0, 0, 0, i)))], [], name,
        4 * len(pairs) * count * wide * units, 4 * len(pairs) * wide * units,
    )[0]


def media_back(grad_pairs, pairs, weights, gain_means, bias_means, gains, media, time_rows, stats, counts, place, frames, patches, groups):
    rows, width = media.shape
    layers = len(pairs)
    turns = len(weights[0])
    wide2 = pairs[0].shape[1]
    chip = width // groups
    half = chip // 2
    group = frames_in_block(frames)
    groups_of = frames // group
    samples = counts.shape[0]

    def body(counts_ref, place_ref, *refs):
        grad_refs = refs[:layers]
        pair_refs = refs[layers : 2 * layers]
        weight_refs = refs[2 * layers : (2 + turns) * layers]
        gm_ref, bm_ref, gain_ref, media_ref, time_ref, stat_ref, mine_ref, theirs_ref = refs[(2 + turns) * layers :]
        part = wide2 // turns
        clip, at = pl.program_id(0), pl.program_id(1)
        for inner in range(group):
            frame = at * group + inner
            here = slice(inner * patches, (inner + 1) * patches)
            live = frame < counts_ref[clip]

            @pl.when(live)
            def _():
                total = jnp.zeros((patches, chip), F32)
                one = jnp.zeros((patches, wide2), F32)
                two = jnp.zeros((patches, wide2), F32)
                for layer in range(layers):
                    grad = grad_refs[layer][here, :]
                    product = jnp.zeros((patches, chip), F32)
                    for turn in range(turns):
                        product += mm_bt(grad[:, turn * part : (turn + 1) * part], weight_refs[layer * turns + turn][...])
                    total = total + product * gain_ref[layer : layer + 1, :]
                    grad = grad.astype(F32)
                    one = one + grad * gm_ref[layer : layer + 1, :]
                    two = two + grad * (pair_refs[layer][here, :].astype(F32) - bm_ref[layer : layer + 1, :])
                mean_one = jnp.sum(one, axis=1, keepdims=True)
                mean_two = jnp.sum(two, axis=1, keepdims=True) * (1.0 / width)
                stat = stat_ref[here, :]
                mean, rstd = stat[:, 0:1], stat[:, 64:65]
                normed = (media_ref[here, :].astype(F32) + time_ref[pl.ds(frame, 1), :] - mean) * rstd
                out = rstd * (total - mean_one - normed * mean_two)
                low, high = out[:, :half], out[:, half:]
                first = place_ref[0] == 0
                mine_ref[here, :] = jnp.where(first, low, high)
                theirs_ref[here, :] = jnp.where(first, high, low)

            @pl.when(jnp.logical_not(live))
            def _():
                mine_ref[here, :] = jnp.zeros((patches, half), F32)
                theirs_ref[here, :] = jnp.zeros((patches, half), F32)

    block = live_block(group, groups_of)

    def chip_block(clip, at, counts_ref, place_ref):
        return (block(clip, at, counts_ref)[0], place_ref[1])

    deep = group * patches
    pair_spec = pl.BlockSpec((deep, wide2), block)
    out_spec = pl.BlockSpec((deep, half), lambda clip, at, *_: (clip * groups_of + at, 0))
    by_chip = lambda count: pl.BlockSpec((count, chip), lambda clip, at, counts_ref, place_ref: (0, place_ref[1]))
    ins = [(value, pair_spec) for value in (*grad_pairs, *pairs)]
    ins += [
        (value, pl.BlockSpec((chip, wide2 // turns), lambda clip, at, counts_ref, place_ref: (place_ref[1], 0)))
        for pieces in weights for value in pieces
    ]
    ins += [
        (gain_means, whole(gain_means.shape)), (bias_means, whole(bias_means.shape)),
        (gains, by_chip(layers)), (media, pl.BlockSpec((deep, chip), chip_block)), (time_rows, by_chip(frames)),
        (stats, pl.BlockSpec((deep, 128), block)),
    ]
    return call(
        body, [counts, place], (samples, groups_of), ins,
        [((rows, half), F32, out_spec)] * 2, [], "media_back",
        2 * rows * wide2 * chip * layers, rows * (wide2 * 4 * layers + 6 * chip),
    )


def media_sum(mine, arrived, frames, patches, samples):
    rows, width = mine.shape
    group = frames_in_block(frames)
    groups = frames // group
    deep = group * patches

    def body(mine_ref, arrived_ref, out_ref, sum_ref):
        clip, at = pl.program_id(0), pl.program_id(1)

        @pl.when((clip == 0) & (at == 0))
        def _():
            sum_ref[...] = jnp.zeros_like(sum_ref)

        total = mine_ref[...] + arrived_ref[...]
        out_ref[...] = total.astype(BF16)
        lines = [jnp.sum(total[i * patches : (i + 1) * patches], axis=0, keepdims=True) for i in range(group)]
        for piece in range(groups):

            @pl.when(at == piece)
            def _():
                for i in range(group):
                    frame = piece * group + i
                    sum_ref[frame : frame + 1, :] += lines[i]

    spec = pl.BlockSpec((deep, width), lambda clip, at: (clip * groups + at, 0))
    return call(
        body, [], (samples, groups), [(mine, spec), (arrived, spec)],
        [((rows, width), BF16, spec), ((frames, width), F32, whole((frames, width)))], [], "media_sum",
        2 * rows * width, 10 * rows * width,
    )


def finish_ff(ups, downs):
    layers = len(ups)
    chunk, units = ups[0][2], ups[0][0].shape[1]

    def body(*refs):
        up_ref, down_ref = refs[2 * layers :]
        for layer in range(layers):
            up_ref[layer] = refs[layer][...]
            down_ref[layer] = jnp.transpose(refs[layers + layer][...], (1, 0))

    ins = [
        (value, pl.BlockSpec((chunk, units), lambda i, at=at: (at, 0))) for value, at, _ in (*ups, *downs)
    ]
    shapes = [(layers, chunk, units), (layers, units, chunk)]
    return call(
        body, [], (1,), ins, [(shape, F32, whole(shape)) for shape in shapes], [], "finish_ff",
        4 * layers * chunk * units, 16 * layers * chunk * units,
    )


def finish_attn(attn, layers, own):
    chunk = attn.shape[1]

    def body(attn_ref, query_ref, key_ref, value_ref, out_ref):
        for layer in range(layers):
            for slot, ref in enumerate((key_ref, value_ref, query_ref, out_ref)):
                at = (4 * layer + slot) * own
                part = attn_ref[at : at + own, :]
                ref[layer] = part if slot == 3 else jnp.transpose(part, (1, 0))

    shapes = [(layers, chunk, own)] * 3 + [(layers, own, chunk)]
    return call(
        body, [], (1,), [(attn, whole(attn.shape))], [(shape, F32, whole(shape)) for shape in shapes], [], "finish_attn",
        attn.size, 8 * attn.size,
    )


class Links:

    def __init__(self, zero):
        self.zero = zero
        self.planes = lax.axis_size("plane")
        self.groups = lax.axis_size("group")
        self.plane = lax.axis_index("plane")
        self.side = lax.axis_index("side")
        self.group = lax.axis_index("group")
        self.core = lax.axis_index("core")

    def rounded(self, value):
        return (value + self.zero).astype(BF16)

    def core_swap(self, value):
        return lax.ppermute(value, "core", [(0, 1), (1, 0)])

    def side_swap(self, value):
        return lax.ppermute(value, "side", [(0, 1), (1, 0)])

    def group_turn(self, value, turn):
        return lax.ppermute(value, "group", [(i, (i + turn) % self.groups) for i in range(self.groups)])

    def cut(self, value, index):
        half = value.shape[0] // 2
        return lax.dynamic_slice_in_dim(value, index * half, half, 0)

    def join(self, mine, other, index):
        first = index == 0
        return jnp.concatenate([jnp.where(first, mine, other), jnp.where(first, other, mine)], axis=0)

    def core_half(self, value):
        return self.cut(value, self.core) + self.core_swap(self.cut(value, 1 - self.core))

    def group_turns(self, value):
        return [self.group_turn(value, k) for k in range(1, self.groups)]

    def group_total(self, value, turned):
        if self.groups == 2:
            return value + turned[0]
        turned = jnp.stack([value] + turned)
        total = None
        for source in range(self.groups):
            slot = lax.rem(self.group - source + self.groups, self.groups)
            term = lax.dynamic_index_in_dim(turned, slot, 0, keepdims=False)
            total = term if total is None else total + term
        return total

    def tensor_halves(self, value):
        mine = self.core_half(value)
        mine = self.group_total(mine, self.group_turns(mine))
        return mine, self.core_swap(mine)

    def dp_sum(self, value):
        value = value + self.side_swap(value)
        step = 1
        while step < self.planes:
            value = value + lax.ppermute(value, "plane", [(i, i ^ step) for i in range(self.planes)])
            step *= 2
        return value

    def columns(self, value, side):
        wide = value.shape[1] // (2 * self.planes)
        cuts = [value[:, i * wide : (i + 1) * wide] for i in range(2 * self.planes)]
        return jnp.where(side == 0, jnp.concatenate(cuts[0::2], axis=1), jnp.concatenate(cuts[1::2], axis=1))

    def both_columns(self, value):
        return self.columns(value, self.side), self.side_swap(self.columns(value, 1 - self.side))

    def scatter(self, value, dimension):
        return lax.psum_scatter(value, "plane", scatter_dimension=dimension, tiled=True)


def local(
    media,
    frame_counts,
    time_embed,
    latents,
    media_gain,
    media_bias,
    latent_gain,
    latent_bias,
    ff_gain,
    ff_bias,
    w_query,
    w_key,
    w_value,
    w_out,
    w_up,
    w_down,
    cotangent,
):
    links = Links(jnp.where(frame_counts[0] > 1000000, 1.0, 0.0).astype(F32))
    samples, media_len, width = media.shape
    frames = time_embed.shape[0]
    patches = media_len // frames
    latent_rows = latents.shape[0]
    own = w_query.shape[2]
    layers = w_query.shape[0]
    wide = own * links.groups
    rows = samples * latent_rows
    tensor_size = 2 * links.groups
    turns = range(1, links.groups)
    place = jnp.stack([links.core, links.group, links.side]).astype(jnp.int32)

    def row(value, depth):
        return value[depth : depth + 1]

    def after(values, event):
        return lax.optimization_barrier((values, event))

    def project(depth, x, pair, weight, nears, fars):
        pieces = [weight]
        for k in turns:
            far = None if fars is None else fars[k - 1]
            pair, weight = project_more(x, frame_counts, place, pair, nears[k - 1], far, k, frames, patches)
            pieces.append(weight)
        return pair, pieces

    def packed(depth, event):
        weights, event = after((w_key, w_value, w_query, w_out), event)
        wanted = [(weights[:2], depth, depth > 0), (weights[2:3], depth, False), (weights[3:], depth, False)]
        return lax.optimization_barrier((pack(place, wanted, "pack"), event))

    def near_of(depth, values):
        for name, value in zip(("pair", "query", "out"), values):
            nears[name, depth] = links.group_turns(value)

    def by_side(nears):
        return [links.side_swap(value) for value in nears]

    def more_of(depth):
        return [(query, None, out, None) for query, out in zip(nears["query", depth], nears["out", depth])]

    media_rows = media.reshape(samples * media_len, width)
    time_rows = time_embed.astype(F32)

    def prepared(depth, media_then):
        return prepare(
            media_then, frame_counts, time_rows, row(media_gain, depth), row(media_bias, depth),
            w_key, w_value, depth, links.groups, frames, patches,
        )

    nears = {}
    media_then = media_rows
    if layers > 1:
        sent, media_then = packed(1, media_rows)
        near_of(1, sent)
    x, stats, pair, weight = prepared(0, media_then)
    media_x, media_pair, w_pairs = [x], [pair], [[weight]]
    fars = {}
    if layers > 1:
        sent, pair = after(nears["pair", 1], pair)
        media_pair[0] = pair
        fars["pair", 1] = by_side(sent)
    more = [[]]

    state_in = (jnp.broadcast_to(latents.astype(F32)[None], (samples, latent_rows, width)).reshape(rows, width),)
    cotangent_rows = cotangent.reshape(rows, width)
    low_cotangent, stats = after(cotangent_rows.astype(BF16).astype(F32), stats)
    upstream_cols = links.both_columns(low_cotangent)
    saved = []
    early = []

    def attended_layer(depth, state_in, more, pieces, pair):
        return attend(
            state_in, place, frame_counts, row(latent_gain, depth), row(latent_bias, depth),
            w_query, w_out, more, pieces, depth, pair, latent_rows, frames, patches,
        )

    for depth in range(layers):
        last = depth == layers - 1
        state, latent_x, queries, lat_pair, attended, log_total, part, query4, out4 = attended_layer(
            depth, state_in, more[depth], w_pairs[depth], media_pair[depth]
        )
        if depth == 0:
            if not last:
                (nears["query", 1], nears["out", 1]), part = after((nears["query", 1], nears["out", 1]), part)
            mine = links.core_half(part)
            if last:
                part = links.tensor_halves(part)
            else:
                media_then, mine = after(media_rows, mine)
                sent, mine = packed(0, mine)
                turned = links.group_turns(mine)
                first_sent = sent[1:]
                x, _, pair, weight = prepared(1, media_then)
                (turned, first_pair), x = after((turned, sent[0]), x)
                nears["pair", 0] = links.group_turns(first_pair)
                mine = links.group_total(mine, turned)
                fars["pair", 1], mine = after(fars["pair", 1], mine)
                part = (mine, links.core_swap(mine))
        else:
            part = (part, links.core_swap(part))
        middle, ff_x, pre, hidden, out_part, *back = feed_forward(
            place, state, *part, row(ff_gain, depth), row(ff_bias, depth),
            w_up, w_down, depth, cotangent_rows if last else None,
        )
        saved.append((state, latent_x, queries, lat_pair, attended, log_total, middle, pre, hidden, query4, out4))
        if last:
            hidden_other = links.side_swap(hidden)
            (ff_x, back[0]), hidden_other = after((ff_x, back[0]), hidden_other)
            early.append((hidden_other, links.both_columns(ff_x.astype(F32))))
            continue
        early.append((hidden, ff_x))
        mine = links.core_half(out_part)
        if depth > 0:
            media_then, mine = after(media_rows, mine)
            x, _, pair, weight = prepared(depth + 1, media_then)
        if depth == 0:
            nears["pair", 0], mine = after(nears["pair", 0], mine)
        (x, fars["pair", depth + 1]), mine = after((x, fars["pair", depth + 1]), mine)
        turned = links.group_turns(mine)
        pair, pieces = project(depth + 1, x, pair, weight, nears["pair", depth + 1], fars["pair", depth + 1])
        turned, pair = after(turned, pair)
        media_x.append(x)
        media_pair.append(pair)
        w_pairs.append(pieces)
        mine = links.group_total(mine, turned)
        if depth == 0:
            first_sent, mine = after(first_sent, mine)
            for name, value in zip(("query", "out"), first_sent):
                gathered = lax.all_gather(value, "group", axis=0, tiled=True)
                nears[name, 0] = [Gathered(gathered, links.groups, k) for k in turns]
        state_in = (middle, mine, links.core_swap(mine))
        upstream_cols, state_in = after(upstream_cols, state_in)
        more.append(more_of(depth + 1))
    sums = links.tensor_halves(out_part)
    sums, hidden_other = after(sums, early[-1][0])
    early[-1] = (hidden_other, early[-1][1])
    resampled = middle + links.join(*sums, links.core)

    upstream = cotangent_rows
    grads = [None] * layers
    gains = [None] * layers
    pair_grads = [None] * layers
    attn_ws = [None] * layers
    units = w_up.shape[2]
    for depth in reversed(range(layers)):
        state, latent_x, queries, lat_pair, attended, log_total, middle, pre, hidden, query4, out4 = saved[depth]
        if depth == layers - 1:
            grad_pre, grad_ffx = back
        else:
            upstream, latent_sums, grad_pre, grad_ffx = feed_back(
                grad_middle, saved[depth + 1][0], grad_x, grad_x_other, row(latent_gain, depth + 1),
                pre, w_up, w_down, depth,
            )
            gains[depth + 1] += (latent_sums[0], latent_sums[1])
            upstream_cols = links.both_columns(upstream.astype(BF16).astype(F32))
            if depth == 0:
                (x, pair), (grad_pre, up_sums) = after((media_x[0], media_pair[0]), (grad_pre, up_sums))
                media_pair[0], w_pairs[0] = project(0, x, pair, w_pairs[0][0], nears["pair", 0], None)
                more[0] = more_of(0)
                _, latent_x, queries, lat_pair, attended, log_total, _, query4, out4 = attended_layer(
                    0, (state,), more[0], w_pairs[0], media_pair[0]
                )
                upstream_cols, queries = after(upstream_cols, queries)
        hidden_other, ff_x_cols = early[depth]
        down = (*upstream_cols, hidden, hidden_other)
        up = (*ff_x_cols, grad_pre, links.side_swap(grad_pre))
        grad_mine, grad_other = links.tensor_halves(grad_ffx)
        if depth == layers - 1:
            down = outer_sums([down], links.planes, "down_sums")
            grad_mine, down = after(grad_mine, down)
            grad_down = links.scatter(down.reshape(-1, units), 0)
            grad_down = (grad_down, 0, grad_down.shape[0])
        else:
            both = outer_sums([down, up], links.planes, "ff_sums")
            grad_mine, both = after(grad_mine, both)
            above, both = after(attn_ws[depth + 1], both)
            attn_ws[depth + 1] = above[0] + links.side_swap(above[1])
            both = links.scatter(both.reshape(-1, units), 0)
            grad_down, grad_up = (both, 0, both.shape[0] // 2), (both, 1, both.shape[0] // 2)
        grad_middle, pair_grads[depth], grad_x, attn_w, sums = attend_back(
            upstream, middle, grad_mine, grad_other, place, frame_counts,
            row(ff_gain, depth), row(media_gain, depth), row(media_bias, depth),
            query4, w_pairs[depth], out4, w_key, w_value, depth, queries, lat_pair, attended, log_total, latent_x,
            media_pair[depth], media_x[depth], latent_rows, frames, patches,
        )
        if depth == layers - 1:
            pre_other, grad_x = after(up[3], grad_x)
            up_sums = outer_sums([(*up[:3], pre_other)], links.planes, "up_sums")
            if depth > 0:
                (hidden, ff_x), up_sums = after(early[depth - 1], up_sums)
                early[depth - 1] = (links.side_swap(hidden), links.both_columns(ff_x.astype(F32)))
            grad_up = links.scatter(up_sums.reshape(-1, units), 0)
            grad_up = (grad_up, 0, grad_up.shape[0])
        grad_x_other = links.core_swap(grad_x)
        attn_ws[depth] = (links.columns(attn_w, links.side), links.columns(attn_w, 1 - links.side))
        grads[depth] = (grad_up, grad_down)
        gains[depth] = (sums[0], sums[1], sums[2], sums[3])
    ending = latent_end(grad_middle, saved[0][0], grad_x, grad_x_other, row(latent_gain, 0), latent_rows)
    gains[0] += (ending[0], ending[1])
    latent_part = ending[8:]
    share = 1.0 / tensor_size
    gains = [(g[2], g[3], g[4] * share, g[5] * share, g[0] * share, g[1] * share) for g in gains]

    core_width = width // tensor_size
    weight_long = [jnp.concatenate(w_pairs[l], axis=1).astype(F32) for l in range(layers)]
    gain_means = jnp.stack([jnp.sum(weight_long[l] * media_gain[l][:, None], axis=0) / width for l in range(layers)])
    bias_means = jnp.stack([jnp.sum(weight_long[l] * media_bias[l][:, None], axis=0) for l in range(layers)])
    (attn_mine, attn_theirs), stats = after(attn_ws[0], stats)
    attn_theirs = links.side_swap(attn_theirs)
    if layers > 1:
        attn_ws[1:], stats = after(attn_ws[1:], stats)
    (stats, *tied) = lax.optimization_barrier((stats, *[value[0] for pair in grads[1:] for value in pair]))
    for depth in range(1, layers):
        grads[depth] = tuple((tied.pop(0), *value[1:]) for value in grads[depth])
    mine, theirs = media_back(
        pair_grads, media_pair, w_pairs, gain_means, bias_means, media_gain, media_rows, time_rows, stats,
        frame_counts, place, frames, patches, links.groups,
    )
    (mine, theirs), attn_theirs = after((mine, theirs), attn_theirs)
    attn_ws[0] = attn_mine + attn_theirs
    media_grad, time_part = media_sum(mine, links.core_swap(theirs), frames, patches, samples)
    media_grad = media_grad.reshape(samples, media_len, core_width)

    def column_cuts(value):
        return [value[:, i * core_width : (i + 1) * core_width] for i in range(tensor_size)]

    def column_cut(value, index):
        return lax.dynamic_slice_in_dim(value, index * core_width, core_width, 1)

    gain_flat = jnp.stack([gains[l][m] for m in range(6) for l in range(layers)])
    by_core = [jnp.concatenate(column_cuts(gain_flat)[c::2], axis=1) for c in range(2)]
    core_mine = jnp.where(links.core == 0, by_core[0], by_core[1])
    core_theirs = jnp.where(links.core == 0, by_core[1], by_core[0])
    gain_share = core_mine + links.core_swap(core_theirs)
    gain_sum = column_cut(gain_share, links.group)
    for turn in turns:
        target = lax.rem(links.group + turn, links.groups)
        gain_sum = gain_sum + links.group_turn(column_cut(gain_share, target), turn)
    latent_share = column_cut(latent_part, links.group * 2 + links.core)
    attn_all, (both_grads, media_grad) = after(jnp.concatenate(attn_ws, axis=0), (grads[0][0][0], media_grad))
    small_in = jnp.concatenate([gain_sum, time_part, latent_share], axis=0)
    small_in, attn_all = after(small_in, attn_all)
    attn = links.scatter(attn_all, 1)
    small = links.dp_sum(small_in)
    swapped = links.core_swap(small)
    pair = jnp.concatenate(
        [jnp.where(links.core == 0, small, swapped), jnp.where(links.core == 0, swapped, small)], axis=1
    )
    turned = jnp.stack([pair] + [links.group_turn(pair, k) for k in turns])
    order = [lax.rem(links.group - source + links.groups, links.groups) for source in range(links.groups)]
    small_all = jnp.concatenate(
        [lax.dynamic_index_in_dim(turned, slot, 0, keepdims=False) for slot in order], axis=1
    )
    gain_all = small_all[: 6 * layers].reshape(6, layers, width)
    time_grad = small_all[6 * layers : 6 * layers + frames]
    latents_grad = small_all[6 * layers + frames :]
    ups, downs = [grads[l][0] for l in range(layers)], [grads[l][1] for l in range(layers)]
    ups[0], downs[0] = (both_grads, *ups[0][1:]), (both_grads, *downs[0][1:])
    w_up_grad, w_down_grad = finish_ff(ups, downs)
    w_query_grad, w_key_grad, w_value_grad, w_out_grad = finish_attn(attn, layers, own)

    return (
        resampled.reshape(samples, latent_rows, width),
        media_grad,
        time_grad,
        latents_grad,
        gain_all[0],
        gain_all[1],
        gain_all[2],
        gain_all[3],
        gain_all[4],
        gain_all[5],
        w_query_grad,
        w_key_grad,
        w_value_grad,
        w_out_grad,
        w_up_grad,
        w_down_grad,
    )


def solution(mesh):
    dp_size, tensor_size = mesh.devices.shape
    split = jax.sharding.Mesh(
        mesh.devices.reshape(dp_size // 2, 2, tensor_size // 2, 2), ("plane", "side", "group", "core")
    )
    dp, tensor = ("plane", "side"), ("group", "core")
    in_specs = (
        P(dp, None, None),
        P(dp),
        P(),
        P(),
        P(),
        P(),
        P(),
        P(),
        P(),
        P(),
        P(None, None, tensor),
        P(None, None, tensor),
        P(None, None, tensor),
        P(None, tensor, None),
        P(None, None, tensor),
        P(None, tensor, None),
        P(dp, None, None),
    )
    out_specs = (
        P(dp, None, None),
        P(dp, None, tensor),
        P(),
        P(),
        P(),
        P(),
        P(),
        P(),
        P(),
        P(),
        P(None, dp, tensor),
        P(None, dp, tensor),
        P(None, dp, tensor),
        P(None, tensor, dp),
        P(None, dp, tensor),
        P(None, tensor, dp),
    )
    return jax.shard_map(local, mesh=split, in_specs=in_specs, out_specs=out_specs, check_vma=False)
```

time: 689 us -> 413 us (0.60)
  Pallas kernels: 0 us -> 218 us
  matrix products: 175 us -> 0 us
  local copies, waits for them, and re-layouts: 130 us -> 17.3 us
  starting transfers between devices: 140 us -> 27.3 us
  other arithmetic: 136 us -> 30.8 us
  between operations: 4.85 us -> 16.4 us
    pallas_call x0 -> x22, Pallas kernels: none -> 218 us  [call(): pl.pallas_call(body, out_shape=[jax.ShapeDtypeStruct(shape, dtype) for sh...]
    dot_general x70 -> x0, matrix products: 175 us -> none  [the longest x34 66.9 us: mm_at(): lax.dot_general(left_side, right_side, (((0,), (0,)), ((), ())), preferre...]
    ppermute x82 -> x41, starting transfers between devices: 140 us -> 26.7 us  [the longest x11 12.3 us: group_turn(): lax.ppermute(value, 'group', [(i, (i + turn) % self.groups) for i in rang...]
    reduce_sum x28 -> x2, other arithmetic: 52.5 us -> 1.92 us  [local(): jnp.sum(weight_long[l] * media_bias[l][:, None], axis=0)]
    reshape x21 -> x0, local copies, waits for them, and re-layouts: 39 us -> none  [the longest x2 10.8 us: local(): grad_value = jnp.einsum('shqk,sqhd->skhd', probs.astype(BF16), grad_heads...]
    slice x40 -> x11, local copies, waits for them, and re-layouts: 31.6 us -> 4.85 us  [the longest x6 2.04 us: columns(): cuts = [value[:, i * wide:(i + 1) * wide] for i in range(2 * self.planes)]]
    unnamed x417 -> x84, local copies, waits for them, and re-layouts: 30.9 us -> 5.71 us
    convert_element_type x22 -> x3, other arithmetic: 20.9 us -> 1.85 us  [the longest x1 1.18 us: local(): upstream_cols = links.both_columns(upstream.astype(BF16).astype(F32))]
  transfers between devices with their start and end apart: 82 -> 47, of which waited for: 17 -> 19; matrix products, arithmetic and copies ran while one was open for 60% -> 10% of each run, Pallas kernels for 0% -> 49%
where the time goes in v2:
time: 413 us; the launch traced here: 409 us
  Pallas kernels  218 us (53%)
  waiting for transfers between devices  99.6 us (24%)
  other arithmetic  30.8 us (7%)
  starting transfers between devices  27.3 us (7%)
  local copies, waits for them, and re-layouts  17.3 us (4%)
  between operations  16.4 us (4%)
    pallas_call x22, Pallas kernels, call(): pl.pallas_call(body, out_shape=[jax.ShapeDtypeStruct(shape, dtype) for sh...  218 us
    ppermute x11, waiting for transfers between devices, group_turn(): lax.ppermute(value, 'group', [(i, (i + turn) % self.groups) for i in rang...  38.1 us
    ppermute x12, waiting for transfers between devices, side_swap(): return lax.ppermute(value, 'side', [(0, 1), (1, 0)])  19 us
    ppermute x2, waiting for transfers between devices, dp_sum(): lax.ppermute(value, 'plane', [(i, i ^ step) for i in range(self.planes)])  18.2 us
    ppermute x11, starting transfers between devices, group_turn(): lax.ppermute(value, 'group', [(i, (i + turn) % self.groups) for i in rang...  12.3 us
    reduce_scatter x4, waiting for transfers between devices, scatter(): lax.psum_scatter(value, 'plane', scatter_dimension=dimension, tiled=True)  12.2 us
    ppermute x16, waiting for transfers between devices, core_swap(): return lax.ppermute(value, 'core', [(0, 1), (1, 0)])  12 us
    ppermute x12, starting transfers between devices, side_swap(): return lax.ppermute(value, 'side', [(0, 1), (1, 0)])  11.7 us
  transfers between devices with their start and end apart: 47, of which 19 were waited for; matrix products, arithmetic and copies ran while one was open for 10% of the time, Pallas kernels for 49%

profile of v2, /device:TPU:0, one launch (start us, length us, event | category | flops | bytes accessed | tf_op | source)
XLA Modules:
  0.0 409.1 jit_solution(8317547111814937980)
XLA Ops:
  8.8 3.0 pack.2
  11.8 3.0 collective-permute-start.1
  14.8 2.0 collective-permute-start.4
  18.6 18.2 %prepare.2 = (bf16[6144,1024]{1,0:T(8,128)(2,1)}, f32[6144,128]{1,0:T(8,128)}, bf16[6144,512]{1,0:T(8,128)(2,1)}, bf16[1024,256]{1,0:T(8,128)(2,1)}) custom-call(s32[3]{0:T(128)} %counts_ref.19, bf16[6144,1024]{1,0:T(8,128)(2,1)} %bitcast.27, f32[8,1024]{1,0:T(8,128)} %convert_element_type.32.time_ref.refs_12_, ...), custom_call_target="tpu_custom_call" | custom-call | flops 3221225472 | bytes 25165824 | tf_op jit(solution)/shard_map/prepare/pallas_call | solution.py:53
  37.9 9.8 %attend.3 = (f32[192,1024]{1,0:T(8,128)}, bf16[192,1024]{1,0:T(8,128)(2,1)}, bf16[192,128]{1,0:T(8,128)(2,1)}, bf16[192,256]{1,0:T(8,128)(2,1)}, f32[192,128]{1,...) custom-call(s32[3]{0:T(128)} %counts_ref.19, ...), custom_call_target="tpu_custom_call" | custom-call | flops 603979776 | bytes 7340032 | tf_op jit(solution)/shard_map/attend/pallas_call | solution.py:53
  47.7 1.6 collective-permute-done.4.refs_8_
  50.7 1.8 collective-permute-start.2
  53.5 3.2 pack.3
  56.7 1.7 collective-permute-start.6
  58.4 18.2 %prepare.3 = (bf16[6144,1024]{1,0:T(8,128)(2,1)}, f32[6144,128]{1,0:T(8,128)}, bf16[6144,512]{1,0:T(8,128)(2,1)}, bf16[1024,256]{1,0:T(8,128)(2,1)}) custom-call(s32[3]{0:T(128)} %counts_ref.19, bf16[6144,1024]{1,0:T(8,128)(2,1)} %bitcast.28, f32[8,1024]{1,0:T(8,128)} %convert_element_type.32.time_ref.refs_12_, ...), custom_call_target="tpu_custom_call" | custom-call | flops 3221225472 | bytes 25165824 | tf_op jit(solution)/shard_map/prepare/pallas_call | solution.py:53
  80.2 7.0 %feed_forward.2 = (f32[192,1024]{1,0:T(8,128)}, bf16[192,1024]{1,0:T(8,128)(2,1)}, f32[192,1024]{1,0:T(8,128)}, f32[192,1024]{1,0:T(8,128)}, f32[192,1024]{1,0:T(8,128)}) custom-call(s32[3]{0:T(128)} %pad_add_fusion.place_ref, f32[192,1024]{1,0:T(8,128)} %get-tuple-element.188.state_ref.refs_0_, f32[96,1024]{1,0:T(8,128)} %copy-done.7, ...), custom_call_target="tpu_custom_call" | custom-call | flops 805306368 | bytes 10092544 | tf_op jit(solution)/shard_map/feed_forward/pallas_call | solution.py:53
  90.2 13.4 %collective-permute-done.8.refs_0_ = f32[1024,256]{1,0:T(8,128)} collective-permute-done((f32[1024,256]{1,0:T(8,128)}, f32[1024,256]{1,0:T(8,128)}, u32[]{:S(2)}, u32[]{:S(2)}) %collective-permute-start.8) | collective-permute-done | bytes 1048608 | tf_op jit(solution)/shard_map/ppermute | solution.py:819
  105.0 11.6 %project_more.2 = (bf16[6144,512]{1,0:T(8,128)(2,1)}, bf16[1024,256]{1,0:T(8,128)(2,1)}) custom-call(s32[3]{0:T(128)} %counts_ref.19, s32[3]{0:T(128)} %pad_add_fusion.place_ref, bf16[6144,1024]{1,0:T(8,128)(2,1)} %get-tuple-element.218.x_ref.refs_10_, bf16[6144,512]{1,0:T(8,128)(2,1)} %get-tuple-element.219.pair_in_ref, ...), custom_call_target="tpu_custom_call", output_to_operand_aliasing={{0}: (3, {})} | custom-call | flops 3221225472 | bytes 15728640 | tf_op jit(solution)/shard_map/project_more/pallas_call | solution.py:53
  116.7 1.7 collective-permute-done.11.refs_2_
  119.2 12.2 %attend.4 = (f32[192,1024]{1,0:T(8,128)}, bf16[192,1024]{1,0:T(8,128)(2,1)}, bf16[192,256]{1,0:T(8,128)(2,1)}, bf16[192,512]{1,0:T(8,128)(2,1)}, f32[192,256]{1,...) custom-call(s32[3]{0:T(128)} %counts_ref.19, ...), custom_call_target="tpu_custom_call" | custom-call | flops 2415919104 | bytes 11534336 | tf_op jit(solution)/shard_map/attend/pallas_call | solution.py:53
  131.9 2.1 collective-permute-done.12.other_ref
  134.9 8.6 %feed_forward.3 = (f32[192,1024]{1,0:T(8,128)}, bf16[192,1024]{1,0:T(8,128)(2,1)}, f32[192,1024]{1,0:T(8,128)}, f32[192,1024]{1,0:T(8,128)}, f32[192,1024]{1,0:T...) custom-call(s32[3]{0:T(128)} %pad_add_fusion.place_ref, f32[192,1024]{1,0:T(8,128)} %get-tuple-element.232.state_ref, ...), custom_call_target="tpu_custom_call" | custom-call | flops 1610612736 | bytes 10092544 | tf_op jit(solution)/shard_map/feed_forward/pallas_call | solution.py:53
  145.0 1.8 collective-permute-start.16
  148.1 1.7 collective-permute-start.14
  149.9 1.6 collective-permute-start.18
  151.5 11.6 %collective-permute-done.14 = f32[96,1024]{1,0:T(8,128)S(1)} collective-permute-done((f32[96,1024]{1,0:T(8,128)S(1)}, f32[96,1024]{1,0:T(8,128)S(1)}, u32[]{:S(2)}, u32[]{:S(2)}) %collective-permute-start.14) | collective-permute-done | bytes 393248 | tf_op jit(solution)/shard_map/ppermute | solution.py:819
  163.2 2.0 collective-permute-done.16.refs_3_
  165.2 6.2 %collective-permute-done.18 = f32[96,1024]{1,0:T(8,128)S(1)} collective-permute-done((f32[96,1024]{1,0:T(8,128)S(1)}, f32[96,1024]{1,0:T(8,128)S(1)}, u32[]{:S(2)}, u32[]{:S(2)}) %collective-permute-start.18) | collective-permute-done | bytes 393248 | tf_op jit(solution)/shard_map/ppermute | solution.py:819
  172.1 3.5 down_sums.1
  179.8 21.2 %attend_back.2 = (f32[192,1024]{1,0:T(8,128)}, bf16[6144,512]{1,0:T(8,128)(2,1)}, f32[192,1024]{1,0:T(8,128)}, f32[512,1024]{1,0:T(8,128)}, f32[8,1024]{1,0:T(8,128)}) custom-call(s32[3]{0:T(128)} %counts_ref.19, s32[3]{0:T(128)} %pad_add_fusion.place_ref, f32[192,1024]{1,0:T(8,128)} %bitcast.34, f32[192,1024]{1,0:T(8,128)} %get-tuple-element.234.mid_ref, ...), custom_call_target="tpu_custom_call" | custom-call | flops 7247757312 | bytes 33030144 | tf_op jit(solution)/shard_map/attend_back/pallas_call | solution.py:53
  201.1 3.7 collective-permute-done.25.refs_1_
  204.7 3.4 up_sums.1
  214.5 7.9 %feed_back.1 = (f32[192,1024]{1,0:T(8,128)}, f32[8,1024]{1,0:T(8,128)}, f32[192,1024]{1,0:T(8,128)}, f32[192,1024]{1,0:T(8,128)}) custom-call(f32[192,1024]{1,0:T(8,128)} %get-tuple-element.254.grad_ref, f32[192,1024]{1,0:T(8,128)} %get-tuple-element.232.state_ref, f32[192,1024]{1,0:T(8,128)} %get-tuple-element.257.gx_ref, ...), custom_call_target="tpu_custom_call" | custom-call | flops 805306368 | bytes 10092544 | tf_op jit(solution)/shard_map/feed_back/pallas_call | solution.py:53
  229.0 11.7 %project_more.3 = (bf16[6144,512]{1,0:T(8,128)(2,1)}, bf16[1024,256]{1,0:T(8,128)(2,1)}) custom-call(s32[3]{0:T(128)} %counts_ref.19, s32[3]{0:T(128)} %pad_add_fusion.place_ref, bf16[6144,1024]{1,0:T(8,128)(2,1)} %get-tuple-element.270.x_ref.refs_10_, bf16[6144,512]{1,0:T(8,128)(2,1)} %get-tuple-element.271.refs_6_.pair_in_ref, ...), custom_call_target="tpu_custom_call", output_to_operand_aliasing={{0}: (3, {})} | custom-call | flops 3221225472 | bytes 15728640 | tf_op jit(solution)/shard_map/project_more/pallas_call | solution.py:53
  240.8 1.9 add.117.mine_ref
  244.3 12.1 %attend.5 = (f32[192,1024]{1,0:T(8,128)}, bf16[192,1024]{1,0:T(8,128)(2,1)}, bf16[192,256]{1,0:T(8,128)(2,1)}, bf16[192,512]{1,0:T(8,128)(2,1)}, f32[192,256]{1,...) custom-call(s32[3]{0:T(128)} %counts_ref.19, ...), custom_call_target="tpu_custom_call" | custom-call | flops 2415919104 | bytes 11534336 | tf_op jit(solution)/shard_map/attend/pallas_call | solution.py:53
  256.3 8.8 %collective-permute-done.24.refs_1_ = f32[192,512]{1,0:T(8,128)} collective-permute-done((f32[192,512]{1,0:T(8,128)}, f32[192,512]{1,0:T(8,128)}, u32[]{:S(2)}, u32[]{:S(2)}) %collective-permute-start.24) | collective-permute-done | bytes 393248 | tf_op jit(solution)/shard_map/ppermute | solution.py:816
  265.2 4.9 %ff_sums.1 = f32[4,2,128,1024]{3,2,1,0:T(8,128)} custom-call(f32[192,512]{1,0:T(8,128)} %get-tuple-element.276.refs_0_, f32[192,512]{1,0:T(8,128)} %collective-permute-done.24.refs_1_, f32[192,1024]{1,0:T(8,128)} %get-tuple-element.278.refs_2_, f32[192,1024]{1,0:T(8,128)} %collective-permute-done.26.refs_3_, f32[192,512]{1,0:T(8,128)} %get-tuple-element.355.refs_4_, ...), custom_call_target="tpu_custom_call" | custom-call | flops 805306368 | bytes 4194304 | tf_op jit(solution)/shard_map/ff_sums/pallas_call | solution.py:53
  271.9 21.5 %attend_back.3 = (f32[192,1024]{1,0:T(8,128)}, bf16[6144,512]{1,0:T(8,128)(2,1)}, f32[192,1024]{1,0:T(8,128)}, f32[512,1024]{1,0:T(8,128)}, f32[8,1024]{1,0:T(8,128)}) custom-call(s32[3]{0:T(128)} %counts_ref.19, s32[3]{0:T(128)} %pad_add_fusion.place_ref, f32[192,1024]{1,0:T(8,128)} %get-tuple-element.259.up_ref, ...), custom_call_target="tpu_custom_call" | custom-call | flops 7247757312 | bytes 33030144 | tf_op jit(solution)/shard_map/attend_back/pallas_call | solution.py:53
  293.4 1.7 fusion.28
  298.3 2.4 add.118
  300.7 23.7 %media_back.1 = (f32[6144,256]{1,0:T(8,128)}, f32[6144,256]{1,0:T(8,128)}) custom-call(s32[3]{0:T(128)} %counts_ref.19, s32[3]{0:T(128)} %pad_add_fusion.place_ref, bf16[6144,512]{1,0:T(8,128)(2,1)} %get-tuple-element.292.refs_0_, bf16[6144,512]{1,0:T(8,128)(2,1)} %get-tuple-element.293.refs_1_, bf16[6144,512]{1,0:T(8,128)(2,1)} %get-tuple-element.274.refs_9_.refs_2_, ...), custom_call_target="tpu_custom_call" | custom-call | flops 6442450944 | bytes 44040192 | tf_op jit(solution)/shard_map/media_back/pallas_call | solution.py:53
  327.7 4.9 %collective-permute-done.33.gy_ref = f32[192,1024]{1,0:T(8,128)S(1)} collective-permute-done((f32[192,1024]{1,0:T(8,128)S(1)}, f32[192,1024]{1,0:T(8,128)S(1)}, u32[]{:S(2)}, u32[]{:S(2)}) %collective-permute-start.33) | collective-permute-done | bytes 786464 | tf_op jit(solution)/shard_map/ppermute | solution.py:813
  333.4 3.3 latent_end.1
  339.7 3.3 collective-permute-done.35
  346.0 7.4 %media_sum.1 = (bf16[6144,256]{1,0:T(8,128)(2,1)}, f32[8,256]{1,0:T(8,128)}) custom-call(f32[6144,256]{1,0:T(8,128)} %get-tuple-element.308.mine_ref, f32[6144,256]{1,0:T(8,128)} %collective-permute-done.32.arrived_ref), custom_call_target="tpu_custom_call" | custom-call | flops 3145728 | bytes 15728640 | tf_op jit(solution)/shard_map/media_sum/pallas_call | solution.py:53
  354.2 4.5 %collective-permute-done.36 = f32[84,256]{1,0:T(8,128)S(1)} collective-permute-done((f32[84,256]{1,0:T(8,128)S(1)}, f32[84,256]{1,0:T(8,128)S(1)}, u32[]{:S(2)}, u32[]{:S(2)}) %collective-permute-start.36) | collective-permute-done | bytes 86048 | tf_op jit(solution)/shard_map/ppermute | solution.py:816
  358.9 8.1 %collective-permute-done.37 = f32[84,256]{1,0:T(8,128)S(1)} collective-permute-done((f32[84,256]{1,0:T(8,128)S(1)}, f32[84,256]{1,0:T(8,128)S(1)}, u32[]{:S(2)}, u32[]{:S(2)}) %collective-permute-start.37) | collective-permute-done | bytes 86048 | tf_op jit(solution)/shard_map/ppermute | solution.py:855
  367.1 10.1 %collective-permute-done.38 = f32[84,256]{1,0:T(8,128)S(1)} collective-permute-done((f32[84,256]{1,0:T(8,128)S(1)}, f32[84,256]{1,0:T(8,128)S(1)}, u32[]{:S(2)}, u32[]{:S(2)}) %collective-permute-start.38) | collective-permute-done | bytes 86048 | tf_op jit(solution)/shard_map/ppermute | solution.py:855
  380.2 3.2 finish_ff.1
  383.4 2.0 collective-permute-done.40
  387.4 12.2 %reduce-scatter.11.cloned.1.call-done.attn_ref = f32[1024,128]{1,0:T(8,128)} async-done(((f32[1024,512]{1,0:T(8,128)}), f32[1024,128]{1,0:T(8,128)}) %reduce-scatter.11.cloned.1.call-update) | async-done | bytes 524304 | tf_op jit(solution)/shard_map/reduce_scatter | solution.py:868
  399.6 1.9 finish_attn.1
  (226 shorter events, 59.4 us)
Async XLA Ops:
  8.1 236.2 %all-gather.3.cloned.1.call-start = ((), (), s32[]{:S(2)}) async-start(), calls=%async_computation.4 | async-start | bytes 1572864 | tf_op jit(solution)/shard_map/all_gather | solution.py:1020
  11.8 25.1 %collective-permute-start.1 = (f32[512,256]{1,0:T(8,128)}, f32[512,256]{1,0:T(8,128)S(1)}, u32[]{:S(2)}, u32[]{:S(2)}) collective-permute-start(f32[512,256]{1,0:T(8,128)} %get-tuple-element.185), channel_id=1, source_target_pairs={{0,2},{2,0},{1,3},{3,1},{4,6},{6,4},{5,7},{7,5},{8,10},{10,8},{9,1... | collective-permute-start | bytes 1572872 | tf_op jit(solution)/shard_map/ppermute | solution.py:819
  14.8 32.9 %collective-permute-start.3 = (f32[1024,128]{1,0:T(8,128)}, f32[1024,128]{1,0:T(8,128)S(1)}, u32[]{:S(2)}, u32[]{:S(2)}) collective-permute-start(f32[1024,128]{1,0:T(8,128)} %get-tuple-element.190), channel_id=1, source_target_pairs={{0,2},{2,0},{1,3},{3,1},{4,6},{6,4},{5,7},{7,5},{8,10},{10,8},{9,1... | collective-permute-start | bytes 1572872 | tf_op jit(solution)/shard_map/ppermute | solution.py:819
  14.8 34.6 %collective-permute-start.4 = (f32[128,1024]{1,0:T(8,128)}, f32[128,1024]{1,0:T(8,128)S(1)}, u32[]{:S(2)}, u32[]{:S(2)}) collective-permute-start(f32[128,1024]{1,0:T(8,128)} %get-tuple-element.191), channel_id=1, source_target_pairs={{0,2},{2,0},{1,3},{3,1},{4,6},{6,4},{5,7},{7,5},{8,10},{10,8},{9,1... | collective-permute-start | bytes 1572872 | tf_op jit(solution)/shard_map/ppermute | solution.py:819
  49.4 27.2 %copy-start.23 = (f32[128,1024]{1,0:T(8,128)}, f32[128,1024]{1,0:T(8,128)S(1)}, u32[]{:S(2)}) copy-start(f32[128,1024]{1,0:T(8,128)S(1)} %collective-permute-done.4.refs_8_) | copy-start | bytes 1572868
  50.6 1.9 collective-permute-start.5
  50.7 27.0 %collective-permute-start.2 = (f32[512,256]{1,0:T(8,128)S(1)}, f32[512,256]{1,0:T(8,128)}, u32[]{:S(2)}, u32[]{:S(2)}) collective-permute-start(f32[512,256]{1,0:T(8,128)S(1)} %collective-permute-done.1.refs_0_), channel_id=1, source_target_pairs={{0,4},{4,0},{1,5},{5,1},{2,6},{6,2},{3,7},{7,3},{8,12},{12,8},{9,1... | collective-permute-start | bytes 1572872 | tf_op jit(solution)/shard_map/ppermute | solution.py:816
  56.7 19.9 %collective-permute-start.6 = (f32[96,1024]{1,0:T(8,128)S(1)}, f32[96,1024]{1,0:T(8,128)}, u32[]{:S(2)}, u32[]{:S(2)}) collective-permute-start(f32[96,1024]{1,0:T(8,128)S(1)} %dynamic-slice_add_fusion.4), channel_id=1, source_target_pairs={{0,2},{2,0},{1,3},{3,1},{4,6},{6,4},{5,7},{7,5},{8,10},{10,8},{9,1... | collective-permute-start | bytes 1179656 | tf_op jit(solution)/shard_map/ppermute | solution.py:819
  77.7 1.8 collective-permute-start.7
  77.8 25.9 %collective-permute-start.8 = (f32[1024,256]{1,0:T(8,128)}, f32[1024,256]{1,0:T(8,128)}, u32[]{:S(2)}, u32[]{:S(2)}) collective-permute-start(f32[1024,256]{1,0:T(8,128)} %get-tuple-element.214), channel_id=1, source_target_pairs={{0,2},{2,0},{1,3},{3,1},{4,6},{6,4},{5,7},{7,5},{8,10},{10,8},{9,1... | collective-permute-start | bytes 3145736 | tf_op jit(solution)/shard_map/ppermute | solution.py:819
  88.4 1.8 collective-permute-start.9
  103.6 12.9 %collective-permute-start.10 = (f32[96,1024]{1,0:T(8,128)S(1)}, f32[96,1024]{1,0:T(8,128)S(1)}, u32[]{:S(2)}, u32[]{:S(2)}) collective-permute-start(f32[96,1024]{1,0:T(8,128)S(1)} %dynamic-slice_add_fusion.3), channel_id=1, source_target_pairs={{0,2},{2,0},{1,3},{3,1},{4,6},{6,4},{5,7},{7,5},{8,10},{10,8},{9,1... | collective-permute-start | bytes 1179656 | tf_op jit(solution)/shard_map/ppermute | solution.py:819
  104.8 11.9 %collective-permute-start = (f32[192,512]{1,0:T(8,128)S(1)}, f32[192,512]{1,0:T(8,128)S(1)}, u32[]{:S(2)}, u32[]{:S(2)}) collective-permute-start(f32[192,512]{1,0:T(8,128)S(1)} %get-tuple-element.370), channel_id=1, source_target_pairs={{0,4},{4,0},{1,5},{5,1},{2,6},{6,2},{3,7},{7,3},{8,12},{12,8},{9,1... | collective-permute-start | bytes 1179656 | tf_op jit(solution)/shard_map/ppermute | solution.py:816
  116.6 1.8 collective-permute-start.11
  131.4 2.6 collective-permute-start.12
  131.7 112.6 %all-gather.5.cloned.1.call-start = ((), (), s32[]{:S(2)}) async-start(), calls=%async_computation.5 | async-start | bytes 1572864 | tf_op jit(solution)/shard_map/all_gather | solution.py:1020
  144.7 3.3 collective-permute-start.13
  145.0 155.7 %reduce-scatter.7.cloned.1.call-start = ((), (), s32[]{:S(2)}) async-start(), calls=%async_computation.7 | async-start | bytes 2621440 | tf_op jit(solution)/shard_map/reduce_scatter | solution.py:868
  145.0 20.1 %collective-permute-start.16 = (f32[192,1024]{1,0:T(8,128)}, f32[192,1024]{1,0:T(8,128)S(1)}, u32[]{:S(2)}, u32[]{:S(2)}) collective-permute-start(f32[192,1024]{1,0:T(8,128)} %get-tuple-element.238.refs_2_), channel_id=1, source_target_pairs={{0,4},{4,0},{1,5},{5,1},{2,6},{6,2},{3,7},{7,3},{8,12},{12,8},{9,1... | collective-permute-start | bytes 2359304 | tf_op jit(solution)/shard_map/ppermute | solution.py:816
  147.9 1.9 collective-permute-start.17
  148.1 14.9 %collective-permute-start.14 = (f32[96,1024]{1,0:T(8,128)S(1)}, f32[96,1024]{1,0:T(8,128)S(1)}, u32[]{:S(2)}, u32[]{:S(2)}) collective-permute-start(f32[96,1024]{1,0:T(8,128)S(1)} %dynamic-slice_add_fusion.2), channel_id=1, source_target_pairs={{0,2},{2,0},{1,3},{3,1},{4,6},{6,4},{5,7},{7,5},{8,10},{10,8},{9,1... | collective-permute-start | bytes 1179656 | tf_op jit(solution)/shard_map/ppermute | solution.py:819
  149.9 21.4 %collective-permute-start.18 = (f32[96,1024]{1,0:T(8,128)S(1)}, f32[96,1024]{1,0:T(8,128)S(1)}, u32[]{:S(2)}, u32[]{:S(2)}) collective-permute-start(f32[96,1024]{1,0:T(8,128)S(1)} %dynamic-slice_add_fusion.1), channel_id=1, source_target_pairs={{0,2},{2,0},{1,3},{3,1},{4,6},{6,4},{5,7},{7,5},{8,10},{10,8},{9,1... | collective-permute-start | bytes 1179656 | tf_op jit(solution)/shard_map/ppermute | solution.py:819
  163.1 9.0 %collective-permute-start.15 = (f32[96,1024]{1,0:T(8,128)S(1)}, f32[96,1024]{1,0:T(8,128)S(1)}, u32[]{:S(2)}, u32[]{:S(2)}) collective-permute-start(f32[96,1024]{1,0:T(8,128)S(1)} %add.112), channel_id=1, source_target_pairs={{0,1},{1,0},{2,3},{3,2},{4,5},{5,4},{6,7},{7,6},{8,9},{9,8},{10,11... | collective-permute-start | bytes 1179656 | tf_op jit(solution)/shard_map/ppermute | solution.py:813
  175.7 125.0 %reduce-scatter.5.cloned.1.call-start = ((), (), s32[]{:S(2)}) async-start(), calls=%async_computation.6 | async-start | bytes 2621440 | tf_op jit(solution)/shard_map/reduce_scatter | solution.py:868
  175.8 4.1 collective-permute-start.19
  176.8 24.2 %collective-permute-start.20 = (f32[192,1024]{1,0:T(8,128)S(1)}, f32[192,1024]{1,0:T(8,128)S(1)}, u32[]{:S(2)}, u32[]{:S(2)}) collective-permute-start(f32[192,1024]{1,0:T(8,128)S(1)} %copy-done.19), channel_id=1, source_target_pairs={{0,4},{4,0},{1,5},{5,1},{2,6},{6,2},{3,7},{7,3},{8,12},{12,8},{9,1... | collective-permute-start | bytes 2359304 | tf_op jit(solution)/shard_map/ppermute | solution.py:816
  179.3 25.4 %collective-permute-start.25 = (f32[192,512]{1,0:T(8,128)}, f32[192,512]{1,0:T(8,128)}, u32[]{:S(2)}, u32[]{:S(2)}) collective-permute-start(f32[192,512]{1,0:T(8,128)} %get-tuple-element.356), channel_id=1, source_target_pairs={{0,4},{4,0},{1,5},{5,1},{2,6},{6,2},{3,7},{7,3},{8,12},{12,8},{9,1... | collective-permute-start | bytes 1179656 | tf_op jit(solution)/shard_map/ppermute | solution.py:816
  208.2 145.2 %reduce-scatter.9.cloned.1.call-start = ((), (), s32[]{:S(2)}) async-start(), calls=%async_computation.8 | async-start | bytes 5242880 | tf_op jit(solution)/shard_map/reduce_scatter | solution.py:868
  209.8 4.7 %collective-permute-start.21 = (f32[192,1024]{1,0:T(8,128)}, f32[192,1024]{1,0:T(8,128)}, u32[]{:S(2)}, u32[]{:S(2)}) collective-permute-start(f32[192,1024]{1,0:T(8,128)} %get-tuple-element.257.gx_ref), channel_id=1, source_target_pairs={{0,1},{1,0},{2,3},{3,2},{4,5},{5,4},{6,7},{7,6},{8,9},{9,8},{10,11... | collective-permute-start | bytes 2359304 | tf_op jit(solution)/shard_map/ppermute | solution.py:813
  211.4 53.8 %collective-permute-start.26 = (f32[192,1024]{1,0:T(8,128)}, f32[192,1024]{1,0:T(8,128)}, u32[]{:S(2)}, u32[]{:S(2)}) collective-permute-start(f32[192,1024]{1,0:T(8,128)} %get-tuple-element.278.refs_2_), channel_id=1, source_target_pairs={{0,4},{4,0},{1,5},{5,1},{2,6},{6,2},{3,7},{7,3},{8,12},{12,8},{9,1... | collective-permute-start | bytes 2359304 | tf_op jit(solution)/shard_map/ppermute | solution.py:816
  214.0 51.2 %collective-permute-start.27 = (f32[192,512]{1,0:T(8,128)}, f32[192,512]{1,0:T(8,128)}, u32[]{:S(2)}, u32[]{:S(2)}) collective-permute-start(f32[192,512]{1,0:T(8,128)} %get-tuple-element.354), channel_id=1, source_target_pairs={{0,4},{4,0},{1,5},{5,1},{2,6},{6,2},{3,7},{7,3},{8,12},{12,8},{9,1... | collective-permute-start | bytes 1179656 | tf_op jit(solution)/shard_map/ppermute | solution.py:816
  223.5 2.9 collective-permute-start.22
  223.6 41.6 %collective-permute-start.28 = (f32[192,1024]{1,0:T(8,128)}, f32[192,1024]{1,0:T(8,128)}, u32[]{:S(2)}, u32[]{:S(2)}) collective-permute-start(f32[192,1024]{1,0:T(8,128)} %get-tuple-element.280.refs_6_), channel_id=1, source_target_pairs={{0,4},{4,0},{1,5},{5,1},{2,6},{6,2},{3,7},{7,3},{8,12},{12,8},{9,1... | collective-permute-start | bytes 2359304 | tf_op jit(solution)/shard_map/ppermute | solution.py:816
  227.2 13.6 %collective-permute-start.23 = (f32[96,1024]{1,0:T(8,128)}, f32[96,1024]{1,0:T(8,128)}, u32[]{:S(2)}, u32[]{:S(2)}) collective-permute-start(f32[96,1024]{1,0:T(8,128)} %dynamic-slice_add_fusion), channel_id=1, source_target_pairs={{0,2},{2,0},{1,3},{3,1},{4,6},{6,4},{5,7},{7,5},{8,10},{10,8},{9,1... | collective-permute-start | bytes 1179656 | tf_op jit(solution)/shard_map/ppermute | solution.py:819
  228.6 36.6 %collective-permute-start.24 = (f32[192,512]{1,0:T(8,128)}, f32[192,512]{1,0:T(8,128)}, u32[]{:S(2)}, u32[]{:S(2)}) collective-permute-start(f32[192,512]{1,0:T(8,128)} %get-tuple-element.358), channel_id=1, source_target_pairs={{0,4},{4,0},{1,5},{5,1},{2,6},{6,2},{3,7},{7,3},{8,12},{12,8},{9,1... | collective-permute-start | bytes 1179656 | tf_op jit(solution)/shard_map/ppermute | solution.py:816
  242.7 29.2 %collective-permute-start.29 = (f32[96,1024]{1,0:T(8,128)}, f32[96,1024]{1,0:T(8,128)}, u32[]{:S(2)}, u32[]{:S(2)}) collective-permute-start(f32[96,1024]{1,0:T(8,128)} %add.117.mine_ref), channel_id=1, source_target_pairs={{0,1},{1,0},{2,3},{3,2},{4,5},{5,4},{6,7},{7,6},{8,9},{9,8},{10,11... | collective-permute-start | bytes 1179656 | tf_op jit(solution)/shard_map/ppermute | solution.py:813
  270.1 28.2 %collective-permute-start.30 = (f32[512,512]{1,0:T(8,128)}, f32[512,512]{1,0:T(8,128)}, u32[]{:S(2)}, u32[]{:S(2)}) collective-permute-start(f32[512,512]{1,0:T(8,128)} %get-tuple-element.297), channel_id=1, source_target_pairs={{0,4},{4,0},{1,5},{5,1},{2,6},{6,2},{3,7},{7,3},{8,12},{12,8},{9,1... | collective-permute-start | bytes 3145736 | tf_op jit(solution)/shard_map/ppermute | solution.py:816
  271.6 128.0 %reduce-scatter.11.cloned.1.call-start = ((), (), s32[]{:S(2)}) async-start(), calls=%async_computation.9 | async-start | bytes 2621440 | tf_op jit(solution)/shard_map/reduce_scatter | solution.py:868
  296.7 27.7 %collective-permute-start.31 = (f32[512,512]{1,0:T(8,128)}, f32[512,512]{1,0:T(8,128)}, u32[]{:S(2)}, u32[]{:S(2)}) collective-permute-start(f32[512,512]{1,0:T(8,128)} %get-tuple-element.304), channel_id=1, source_target_pairs={{0,4},{4,0},{1,5},{5,1},{2,6},{6,2},{3,7},{7,3},{8,12},{12,8},{9,1... | collective-permute-start | bytes 3145736 | tf_op jit(solution)/shard_map/ppermute | solution.py:816
  324.4 21.6 %collective-permute-start.32 = (f32[6144,256]{1,0:T(8,128)}, f32[6144,256]{1,0:T(8,128)}, u32[]{:S(2)}, u32[]{:S(2)}) collective-permute-start(f32[6144,256]{1,0:T(8,128)} %get-tuple-element.309), channel_id=1, source_target_pairs={{0,1},{1,0},{2,3},{3,2},{4,5},{5,4},{6,7},{7,6},{8,9},{9,8},{10,11... | collective-permute-start | bytes 18874376 | tf_op jit(solution)/shard_map/ppermute | solution.py:813
  324.5 8.1 %collective-permute-start.33 = (f32[192,1024]{1,0:T(8,128)S(1)}, f32[192,1024]{1,0:T(8,128)S(1)}, u32[]{:S(2)}, u32[]{:S(2)}) collective-permute-start(f32[192,1024]{1,0:T(8,128)S(1)} %copy-done.13), channel_id=1, source_target_pairs={{0,1},{1,0},{2,3},{3,2},{4,5},{5,4},{6,7},{7,6},{8,9},{9,8},{10,11... | collective-permute-start | bytes 2359304 | tf_op jit(solution)/shard_map/ppermute | solution.py:813
  337.7 1.4 collective-permute-start.34
  339.2 3.8 collective-permute-start.35
  354.2 4.6 %collective-permute-start.36 = (f32[84,256]{1,0:T(8,128)S(1)}, f32[84,256]{1,0:T(8,128)S(1)}, u32[]{:S(2)}, u32[]{:S(2)}) collective-permute-start(f32[84,256]{1,0:T(8,128)S(1)} %pad_maximum_fusion.16), channel_id=1, source_target_pairs={{0,4},{4,0},{1,5},{5,1},{2,6},{6,2},{3,7},{7,3},{8,12},{12,8},{9,1... | collective-permute-start | bytes 258056 | tf_op jit(solution)/shard_map/ppermute | solution.py:816
  358.8 8.2 %collective-permute-start.37 = (f32[84,256]{1,0:T(8,128)S(1)}, f32[84,256]{1,0:T(8,128)S(1)}, u32[]{:S(2)}, u32[]{:S(2)}) collective-permute-start(f32[84,256]{1,0:T(8,128)S(1)} %add.127), channel_id=1, source_target_pairs={{0,8},{8,0},{16,24},{24,16},{1,9},{9,1},{17,25},{25,17},{2,10},{10... | collective-permute-start | bytes 258056 | tf_op jit(solution)/shard_map/ppermute | solution.py:855
  367.0 10.3 %collective-permute-start.38 = (f32[84,256]{1,0:T(8,128)S(1)}, f32[84,256]{1,0:T(8,128)S(1)}, u32[]{:S(2)}, u32[]{:S(2)}) collective-permute-start(f32[84,256]{1,0:T(8,128)S(1)} %add.128), channel_id=1, source_target_pairs={{0,16},{8,24},{16,0},{24,8},{1,17},{9,25},{17,1},{25,9},{2,18},{10... | collective-permute-start | bytes 258056 | tf_op jit(solution)/shard_map/ppermute | solution.py:855
  377.2 1.4 collective-permute-start.39
  378.7 6.7 %collective-permute-start.40 = (f32[84,512]{1,0:T(8,128)S(1)}, f32[84,512]{1,0:T(8,128)S(1)}, u32[]{:S(2)}, u32[]{:S(2)}) collective-permute-start(f32[84,512]{1,0:T(8,128)S(1)} %get-tuple-element.406), channel_id=1, source_target_pairs={{0,2},{2,0},{1,3},{3,1},{4,6},{6,4},{5,7},{7,5},{8,10},{10,8},{9,1... | collective-permute-start | bytes 516104 | tf_op jit(solution)/shard_map/ppermute | solution.py:819
  (41 other events, 347.0 us)
Sparse Core Ops, SparseCore 0:
  131.8 26.1 all-gather.2
  159.6 25.6 all-gather.4
Sparse Core Ops, SparseCore 1:
  175.8 43.5 reduce-scatter.6
  221.6 42.7 reduce-scatter.4
  271.7 75.8 reduce-scatter.8
  354.2 45.3 reduce-scatter.10
